TPU v7x, 128 devices: a whole 4x4x4 slice. The times are simulated.
128 devices in a mesh: ex: 16 (over y_lo, x, core), ey: 8 (over y_hi, z).
Axes of the slice: x: 4, y: 4 (y_hi: 2, y_lo: 2; y = y_hi * 2 + y_lo), z: 4, core: 2. Of those that a mesh axis runs over, the one named last changes fastest.
Arguments:
- settings: float32 [512, 16], replicated, may hold values from -1 to 1
- frequencies: float32 [16, 2048], replicated, may hold values from -4 to 4
- phases: float32 [2048], replicated, may hold values from -3.140625 to 3.140625
- noise_var: float32 [128], replicated, may hold values from 0.01 to 0.1
- signal_scale: float32 [128], replicated, may hold values from 0.5 to 2
- cov_factor: bfloat16 [256, 2048, 2048], P(('ex', 'ey')), as said below
- post_mean: bfloat16 [256, 2048, 128], P(('ex', 'ey')), may hold values from -6 to 6
- component_basis: bfloat16 [128, 1048576], P('ey', 'ex'), may hold values from -0.5 to 0.5
- mean_field: float32 [1048576], P(('ex', 'ey')), may hold values from -4 to 4
Outputs:
- carbon: bfloat16 [512, 1048576], P(None, ('ex', 'ey'))
Inputs may be any that keep to these rules, and one draw needn't show every extreme that they name: `cov_factor`: entries of expert k's factor lie within 8 / sqrt(log(2049)) of zero.
All inputs are finite; a program needn't handle non-finite values.
Results may differ from a plain program's by a relative error of at most 0.0037.
Values may be sent and summed in bfloat16 or wider, within the bound.
No kernel may reach another device: no remote copies, remote signals or barrier semaphores. Data moves between devices by JAX's collectives and lax.ppermute only.
A program may use at most 128 MiB of HBM per device.

v0:
```python
import jax
import jax.numpy as jnp
from jax import lax
from jax.sharding import PartitionSpec as P


def feature_map(settings, frequencies, phases):
    argument = jnp.dot(
        settings, frequencies, precision=lax.Precision.HIGHEST, preferred_element_type=jnp.float32
    )
    scaling = jnp.sqrt(2.0 / frequencies.shape[1])
    return (scaling * jnp.cos(argument + phases[None, :])).astype(jnp.bfloat16)


def per_device(
    settings,
    frequencies,
    phases,
    noise_var,
    signal_scale,
    cov_factor,
    post_mean,
    component_basis,
    mean_field,
):
    relaid = lax.all_to_all(component_basis, "ey", split_axis=1, concat_axis=0, tiled=True)
    feature_rows = feature_map(settings, frequencies, phases)
    feature_float = feature_rows.astype(jnp.float32)
    feature_norm = jnp.sum(feature_float * feature_float, axis=1)
    prior_var = noise_var[None, :] + signal_scale[None, :] * feature_norm[:, None]
    numerator = jnp.zeros(prior_var.shape, jnp.float32)
    precision = jnp.zeros(prior_var.shape, jnp.float32)
    for expert in range(cov_factor.shape[0]):
        projected = jnp.dot(feature_rows, cov_factor[expert], preferred_element_type=jnp.float32)
        spread = jnp.sum(projected * projected, axis=1)
        expert_mean = jnp.dot(feature_rows, post_mean[expert], preferred_element_type=jnp.float32)
        variance = noise_var[None, :] + signal_scale[None, :] * spread[:, None]
        robust_weight = jnp.maximum(0.5 * (jnp.log(prior_var) - jnp.log(variance)), 0.0)
        numerator = numerator + robust_weight / variance * expert_mean
        precision = precision + robust_weight * (1.0 / variance - 1.0 / prior_var)
    total_numer, total_precis = lax.psum((numerator, precision), ("ex", "ey"))
    weights = (total_numer / (total_precis + 1.0 / prior_var)).astype(jnp.bfloat16)
    stock = jnp.dot(weights, relaid, preferred_element_type=jnp.float32) + mean_field[None, :]
    return stock.astype(jnp.bfloat16)


def solution(mesh):
    in_specs = (
        P(),
        P(),
        P(),
        P(),
        P(),
        P(("ex", "ey"), None, None),
        P(("ex", "ey"), None, None),
        P("ey", "ex"),
        P(("ex", "ey")),
    )
    out_specs = P(None, ("ex", "ey"))
    return jax.shard_map(
        per_device, mesh=mesh, in_specs=in_specs, out_specs=out_specs, check_vma=False
    )
```

profile of v0, /device:TPU:1, one launch (start us, length us, event | category | flops | bytes accessed | tf_op | source)
XLA Modules:
  0.0 215.7 jit_solution(3861798324710856279)
XLA Ops:
  6.5 0.0 copy-start
  6.5 0.0 copy-start.5
  6.5 0.0 copy-start.6
  6.5 3.1 %copy.14 = bf16[2,8,8,8192]{3,2,0,1:T(8,128)(2,1)} copy(bf16[2,8,8,8192]{3,2,1,0:T(8,128)(2,1)} %bitcast.31) | data formatting | bytes 4194304 | tf_op jit(solution)/shard_map/all_to_all | solution.py:26
  9.7 8.5 %all-to-all-start = ((bf16[16,8,8192]{2,0,1:T(8,128)(2,1)}), bf16[16,8,8192]{2,0,1:T(8,128)(2,1)S(1)}, u32[]{:S(2)}, u32[]{:S(2)}) async-start(bf16[16,8,8192]{2,0,1:T(8,128)(2,1)} %bitcast.29), calls=%async_computation | async-start | bytes 4194304 | tf_op jit(solution)/shard_map/all_to_all | solution.py:26
  18.2 0.0 all-reduce.3.cloned.1.call-start
  18.2 0.0 copy-done
  18.2 0.0 copy-done.5
  18.2 0.0 copy-done.6
  18.2 0.0 slice-start
  18.3 19.6 %multiply_reduce_fusion.2 = (f32[512]{0:T(512)S(1)}, bf16[512,2048]{1,0:T(8,128)(2,1)S(1)}) fusion(f32[2048]{0:T(1024)S(1)} %copy-done.6, f32[512,16]{0,1:T(8,128)S(1)} %copy-done.5, f32[16,2048]{1,0:T(8,128)S(1)} %copy-done), kind=kOutput, calls=%fused_computation.9 | convolution fusion | flops 207617536 | bytes 2271232 | tf_op jit(solution)/shard_map/dot_general | solution.py:8
  37.8 0.0 slice-start.1
  37.8 0.0 slice-start.2
  37.9 0.0 slice-start.3
  37.9 8.4 %multiply_reduce_fusion = f32[512]{0:T(512)S(1)} fusion(bf16[512,2048]{1,0:T(8,128)(2,1)S(1)} %get-tuple-element.8, bf16[2,2048,2048]{2,1,0:T(8,128)(2,1)} %param.14), kind=kOutput, calls=%fused_computation.7 | convolution fusion | flops 4297063936 | bytes 10487808 | tf_op jit(solution)/shard_map/dot_general | solution.py:34
  46.3 0.0 slice-done
  46.3 0.0 slice-done.1
  46.3 0.0 slice-done.2
  46.3 0.0 slice-done.3
  46.3 0.0 copy-start.2
  46.4 0.0 copy-start.3
  46.4 0.0 copy-start.4
  46.4 4.9 %multiply_reduce_fusion.1 = f32[512]{0:T(512)S(1)} fusion(bf16[512,2048]{1,0:T(8,128)(2,1)S(1)} %get-tuple-element.8, bf16[2,2048,2048]{2,1,0:T(8,128)(2,1)S(1)} %bitcast.33), kind=kOutput, calls=%fused_computation.8 | convolution fusion | flops 4297063936 | bytes 10487808 | tf_op jit(solution)/shard_map/dot_general | solution.py:34
  51.3 0.0 copy-done.2
  51.3 0.0 copy-done.3
  51.3 1.0 multiply_add_fusion
  52.3 0.0 copy-done.4
  52.3 0.0 copy-start.1
  52.3 0.7 convolution_multiply_fusion.1
  53.0 1.4 fusion.10
  54.4 0.0 all-reduce.3.cloned.1.call-update
  54.4 147.5 %all-reduce.3.cloned.1.call-done = (f32[512,128]{1,0:T(8,128)}, f32[512,128]{1,0:T(8,128)}) async-done(((f32[512,128]{1,0:T(8,128)}, f32[512,128]{1,0:T(8,128)}), (f32[512,128]{1,0:T(8,128)}, f32[512,128]{1,0:T(8,128)})) %all-reduce.3.cloned.1.call-update) | async-done | bytes 524304 | tf_op jit(solution)/shard_map/psum | solution.py:41
  202.0 0.0 all-to-all-done
  202.0 0.0 copy-done.1
  202.0 6.8 %add_convert_fusion = bf16[512,8192]{1,0:T(8,128)(2,1)} fusion(bf16[128,8192]{1,0:T(8,128)(2,1)S(1)} %bitcast.30, f32[8192]{0:T(1024)S(1)} %copy-done.1, f32[512,128]{1,0:T(8,128)} %get-tuple-element.5, f32[512,128]{1,0:T(8,128)} %get-tuple-element.6, f32[512]{0:T(512)S(1)} %get-tuple-element.7, f32[128]{0:T(128)S(1)} %copy-done.2, f32[128]{0:T(128)S(1)} %copy-done.3), kind=kOutput, calls=%fused_computation | convolution fusion | flops 1082523648 | bytes 11045888 | tf_op jit(solution)/shard_map/dot_general | solution.py:43
  (1 shorter events, 0.0 us)
Async XLA Ops:
  6.5 11.7 %copy-start = (f32[16,2048]{1,0:T(8,128)S(1)}, f32[16,2048]{1,0:T(8,128)}, u32[]{:S(2)}) copy-start(f32[16,2048]{1,0:T(8,128)} %param.10) | copy-start | bytes 393220
  6.5 11.7 %copy-start.5 = (f32[512,16]{0,1:T(8,128)S(1)}, f32[512,16]{0,1:T(8,128)}, u32[]{:S(2)}) copy-start(f32[512,16]{0,1:T(8,128)} %param.9) | copy-start | bytes 98308
  6.5 11.7 %copy-start.6 = (f32[2048]{0:T(1024)S(1)}, f32[2048]{0:T(1024)}, u32[]{:S(2)}) copy-start(f32[2048]{0:T(1024)} %param.11) | copy-start | bytes 24580
  9.7 192.3 %all-to-all-start = ((bf16[16,8,8192]{2,0,1:T(8,128)(2,1)}), bf16[16,8,8192]{2,0,1:T(8,128)(2,1)S(1)}, u32[]{:S(2)}, u32[]{:S(2)}) async-start(bf16[16,8,8192]{2,0,1:T(8,128)(2,1)} %bitcast.29), calls=%async_computation | async-start | bytes 4194304 | tf_op jit(solution)/shard_map/all_to_all | solution.py:26
  18.2 183.8 %all-reduce.3.cloned.1.call-start = ((), (), s32[]{:S(2)}) async-start(), calls=%async_computation.1 | async-start | bytes 1048576 | tf_op jit(solution)/shard_map/psum | solution.py:41
  18.2 28.1 %slice-start = ((s8[16777216]{0:T(1024)(128)(4,1)}), s8[4194304]{0:T(1024)(128)(4,1)S(1)}, s32[]{:S(2)}) async-start(s8[16777216]{0:T(1024)(128)(4,1)} %bitcast.32), calls=%async_computation.2 | async-start | bytes 8388608
  37.8 8.5 %slice-start.1 = ((s8[16777216]{0:T(1024)(128)(4,1)}), s8[4194304]{0:T(1024)(128)(4,1)S(1)}, s32[]{:S(2)}) async-start(s8[16777216]{0:T(1024)(128)(4,1)} %bitcast.32), calls=%async_computation.3 | async-start | bytes 8388608
  37.8 8.5 %slice-start.2 = ((s8[16777216]{0:T(1024)(128)(4,1)}), s8[4194304]{0:T(1024)(128)(4,1)S(1)}, s32[]{:S(2)}) async-start(s8[16777216]{0:T(1024)(128)(4,1)} %bitcast.32), calls=%async_computation.4 | async-start | bytes 8388608
  37.9 8.5 %slice-start.3 = ((s8[16777216]{0:T(1024)(128)(4,1)}), s8[4194304]{0:T(1024)(128)(4,1)S(1)}, s32[]{:S(2)}) async-start(s8[16777216]{0:T(1024)(128)(4,1)} %bitcast.32), calls=%async_computation.5 | async-start | bytes 8388608
  46.3 4.9 %copy-start.2 = (f32[128]{0:T(128)S(1)}, f32[128]{0:T(128)}, u32[]{:S(2)}) copy-start(f32[128]{0:T(128)} %param.13) | copy-start | bytes 1540
  46.4 4.9 %copy-start.3 = (f32[128]{0:T(128)S(1)}, f32[128]{0:T(128)}, u32[]{:S(2)}) copy-start(f32[128]{0:T(128)} %param.12) | copy-start | bytes 1540
  46.4 5.9 %copy-start.4 = (bf16[2,2048,128]{2,1,0:T(8,128)(2,1)S(1)}, bf16[2,2048,128]{2,1,0:T(8,128)(2,1)}, u32[]{:S(2)}) copy-start(bf16[2,2048,128]{2,1,0:T(8,128)(2,1)} %param.15) | copy-start | bytes 3145732
  52.3 149.7 %copy-start.1 = (f32[8192]{0:T(1024)S(1)}, f32[8192]{0:T(1024)}, u32[]{:S(2)}) copy-start(f32[8192]{0:T(1024)} %param.17) | copy-start | bytes 98308
Sparse Core Ops, SparseCore 0:
  54.6 147.3 all-reduce.2
where the time goes:
time: 216 us
  waiting for transfers between devices  148 us (69%)
  matrix products  41.8 us (19%)
  between operations  13.6 us (6%)
  starting transfers between devices  8.53 us (4%)
  local copies, waits for them, and re-layouts  3.19 us (1%)
    psum x1, waiting for transfers between devices, per_device(): total_numer, total_precis = lax.psum((numerator, precision), ('ex', 'ey'))  148 us
    dot_general x1, matrix products, feature_map(): jnp.dot(settings, frequencies, precision=lax.Precision.HIGHEST, preferred...  19.6 us
    dot_general x2, matrix products, per_device(): jnp.dot(feature_rows, cov_factor[expert], preferred_element_type=jnp.floa...  13.3 us
    all_to_all x1, starting transfers between devices, per_device(): lax.all_to_all(component_basis, 'ey', split_axis=1, concat_axis=0, tiled=...  8.49 us
    dot_general x1, matrix products, per_device(): jnp.dot(weights, relaid, preferred_element_type=jnp.float32)  6.84 us
  transfers between devices with their start and end apart: 2, of which 1 were waited for; matrix products, arithmetic and copies ran while one was open for 17% of the time, Pallas kernels for 0%

commit v1 on v0

v1 whole, which is shorter than its diff:
```python
import functools
import math

import jax
import jax.numpy as jnp
import numpy as np
from jax import lax
from jax.experimental import pallas as pl
from jax.experimental.pallas import tpu as pltpu
from jax.sharding import PartitionSpec as P

AXES = ("ex", "ey")
COLUMNS = 512
ROWS = 32
LANES = 128


def sine_coefficients(terms):
    nodes = 64
    square = (1 / 16) * (0.5 + 0.5 * np.cos((2 * np.arange(nodes) + 1) * np.pi / (2 * nodes)))
    w = np.sqrt(square)
    powers = np.stack([square**i for i in range(terms)], 1) * w[:, None]
    fit, *_ = np.linalg.lstsq(powers, np.sin(2 * np.pi * w), rcond=None)
    return [float(c) for c in fit]


def split(values):
    high = values.astype(jnp.bfloat16)
    rest = values - high.astype(jnp.float32)
    middle = rest.astype(jnp.bfloat16)
    low = (rest - middle.astype(jnp.float32)).astype(jnp.bfloat16)
    return high, middle, low


def experts_kernel(
    devices,
    settings_hbm,
    frequencies_hbm,
    phases_hbm,
    noise_hbm,
    scale_hbm,
    factor_hbm,
    mean_hbm,
    out_ref,
    settings,
    frequencies,
    phases,
    noise,
    scale,
    factor,
    means,
    phi,
    argument,
    squares,
    small_sems,
    sems,
):
    experts, feats, _ = factor.shape
    rows = phi.shape[0]
    chunks = feats // COLUMNS
    small = [
        pltpu.make_async_copy(source, target, small_sems.at[i])
        for i, (source, target) in enumerate(
            (
                (settings_hbm, settings),
                (frequencies_hbm, frequencies),
                (phases_hbm, phases),
                (noise_hbm, noise),
                (scale_hbm, scale),
                (mean_hbm, means),
            )
        )
    ]
    large = [
        pltpu.make_async_copy(
            factor_hbm.at[e, :, pl.ds(n * COLUMNS, COLUMNS)],
            factor.at[e, :, pl.ds(n * COLUMNS, COLUMNS)],
            sems.at[e * chunks + n],
        )
        for e in range(experts)
        for n in range(chunks)
    ]
    for copy in small[:5] + large + small[5:]:
        copy.start()
    for copy in small[:5]:
        copy.wait()

    turn = 1.0 / (2.0 * math.pi)
    a0, a1, a2 = split(settings[...])
    b0, b1, b2 = split(frequencies[...] * turn)
    argument[...] = lax.dot_general(
        jnp.concatenate([a0, a0, a1, a1, a0, a2], 0),
        jnp.concatenate([b0, b1, b0, b1, b2, b0], 0),
        (((0,), (0,)), ((), ())),
        preferred_element_type=jnp.float32,
    )
    amplitude = math.sqrt(2.0 / feats)
    coefficients = [c * amplitude for c in sine_coefficients(5)]

    def feature_rows(r, carry):
        block = pl.ds(pl.multiple_of(r * ROWS, ROWS), ROWS)
        total = jnp.zeros((ROWS, LANES), jnp.float32)
        for c in range(feats // 512):
            span = slice(c * 512, (c + 1) * 512)
            turns = argument[block, span] + phases[:, span] * turn
            turns = turns - jnp.round(turns)
            w = 0.25 - jnp.abs(turns)
            square = w * w
            poly = coefficients[-1]
            for coefficient in coefficients[-2::-1]:
                poly = poly * square + coefficient
            value = (poly * w).astype(jnp.bfloat16)
            phi[block, span] = value
            wide = value.astype(jnp.float32)
            wide = wide * wide
            for j in range(4):
                total = total + wide[:, j * LANES : (j + 1) * LANES]
        squares[experts, block, :] = total
        return carry

    lax.fori_loop(0, rows // ROWS, feature_rows, 0)

    for e in range(experts):
        for n in range(chunks):
            large[e * chunks + n].wait()
            projected = jnp.dot(
                phi[...],
                factor[e, :, n * COLUMNS : (n + 1) * COLUMNS],
                preferred_element_type=jnp.float32,
            )
            projected = projected * projected
            total = projected[:, :LANES]
            for j in range(1, COLUMNS // LANES):
                total = total + projected[:, j * LANES : (j + 1) * LANES]
            squares[e] = total if n == 0 else squares[e] + total
    small[5].wait()

    low_half = lax.broadcasted_iota(jnp.int32, (1, 8, LANES), 1) < 4
    step = 128
    for m in range(rows // step):
        block = slice(m * step, (m + 1) * step)
        prior = noise[...] + scale[...] * jnp.sum(squares[experts, block, :], axis=1, keepdims=True)
        log_prior = jnp.log(prior)
        inv_prior = 1.0 / prior
        numer = jnp.zeros((step, LANES), jnp.float32)
        denom = inv_prior * (1.0 / devices)
        for e in range(experts):
            variance = noise[...] + scale[...] * jnp.sum(squares[e, block, :], axis=1, keepdims=True)
            mean = jnp.dot(phi[block, :], means[e], preferred_element_type=jnp.float32)
            robust = jnp.maximum(0.5 * (log_prior - jnp.log(variance)), 0.0)
            inv_variance = 1.0 / variance
            numer = numer + robust * inv_variance * mean
            denom = denom + robust * (inv_variance - inv_prior)
        numer = numer.reshape(step // 8, 8, LANES)
        denom = denom.reshape(step // 8, 8, LANES)
        tiles = slice(m * step // 8, (m + 1) * step // 8)
        out_ref[tiles, 0] = jnp.where(low_half, numer, pltpu.roll(denom, 4, 1))
        out_ref[tiles, 1] = jnp.where(low_half, pltpu.roll(numer, 4, 1), denom)


def experts_sums(devices, settings, frequencies, phases, noise_var, signal_scale, cov_factor, post_mean):
    experts, feats, _ = cov_factor.shape
    rows, params = settings.shape
    comps = noise_var.shape[0]
    f32, bf16 = jnp.float32, jnp.bfloat16
    sums = pl.pallas_call(
        functools.partial(experts_kernel, devices),
        out_shape=jax.ShapeDtypeStruct((rows // 8, 2, 8, comps), f32),
        in_specs=[pl.BlockSpec(memory_space=pltpu.HBM)] * 7,
        out_specs=pl.BlockSpec(memory_space=pltpu.VMEM),
        scratch_shapes=[
            pltpu.VMEM((params, rows), f32),
            pltpu.VMEM((params, feats), f32),
            pltpu.VMEM((1, feats), f32),
            pltpu.VMEM((1, comps), f32),
            pltpu.VMEM((1, comps), f32),
            pltpu.VMEM((experts, feats, feats), bf16),
            pltpu.VMEM((experts, feats, comps), bf16),
            pltpu.VMEM((rows, feats), bf16),
            pltpu.VMEM((rows, feats), f32),
            pltpu.VMEM((experts + 1, rows, comps), f32),
            pltpu.SemaphoreType.DMA((6,)),
            pltpu.SemaphoreType.DMA((experts * (feats // COLUMNS),)),
        ],
        compiler_params=pltpu.CompilerParams(vmem_limit_bytes=60 * 2**20),
        cost_estimate=pl.CostEstimate(
            flops=2 * experts * rows * feats * (feats + comps),
            bytes_accessed=2 * experts * feats * (feats + comps),
            transcendentals=0,
        ),
    )(
        settings.T,
        frequencies,
        phases[None, :],
        noise_var[None, :],
        signal_scale[None, :],
        cov_factor,
        post_mean,
    )
    return sums.reshape(rows // 4, 8, comps)


def per_device(
    devices,
    settings,
    frequencies,
    phases,
    noise_var,
    signal_scale,
    cov_factor,
    post_mean,
    component_basis,
    mean_field,
):
    relaid = lax.all_to_all(component_basis, "ey", split_axis=1, concat_axis=0, tiled=True)
    sums = experts_sums(
        devices, settings, frequencies, phases, noise_var, signal_scale, cov_factor, post_mean
    )
    relaid, sums = lax.optimization_barrier((relaid, sums))
    parts = lax.all_to_all(sums, AXES, split_axis=0, concat_axis=0, tiled=True)
    total = jnp.sum(parts, axis=0)
    mine = (total[:4] / total[4:]).astype(jnp.bfloat16)
    copies = jnp.broadcast_to(mine[None], (devices,) + mine.shape)
    weights = lax.all_to_all(copies, AXES, split_axis=0, concat_axis=0, tiled=True)
    weights = weights.reshape(settings.shape[0], noise_var.shape[0])
    stock = jnp.dot(weights, relaid, preferred_element_type=jnp.float32) + mean_field[None, :]
    return stock.astype(jnp.bfloat16)


def solution(mesh):
    in_specs = (
        P(),
        P(),
        P(),
        P(),
        P(),
        P(AXES, None, None),
        P(AXES, None, None),
        P("ey", "ex"),
        P(AXES),
    )
    out_specs = P(None, AXES)
    return jax.shard_map(
        functools.partial(per_device, mesh.size),
        mesh=mesh,
        in_specs=in_specs,
        out_specs=out_specs,
        check_vma=False,
    )
```

time: 216 us -> 79 us (0.37)
  waiting for transfers between devices: 148 us -> 6.2 us
  matrix products: 41.8 us -> 5.73 us
  blocking collectives: 0 us -> 35 us
  Pallas kernels: 0 us -> 19.9 us
  between operations: 13.6 us -> 0.02 us
    psum x1 -> x0, waiting for transfers between devices: 148 us -> none  [per_device(): total_numer, total_precis = lax.psum((numerator, precision), ('ex', 'ey'))]
    all_to_all x0 -> x2, blocking collectives: none -> 35 us  [the longest x1 20.3 us: per_device(): parts = lax.all_to_all(sums, AXES, split_axis=0, concat_axis=0, tiled=True)]
    dot_general x5 -> x0, matrix products: 35 us -> none  [the longest x1 19.6 us: feature_map(): jnp.dot(settings, frequencies, precision=lax.Precision.HIGHEST, preferred...]
    pallas_call x0 -> x1, Pallas kernels: none -> 19.9 us  [experts_sums(): pl.pallas_call(functools.partial(experts_kernel, devices), out_shape=jax....]
    all_to_all x1, waiting for transfers between devices: 0.01 us -> 6.2 us  [per_device(): lax.all_to_all(component_basis, 'ey', split_axis=1, concat_axis=0, tiled=...]
  transfers between devices with their start and end apart: 2 -> 1, of which waited for: 1 -> 1; matrix products, arithmetic and copies ran while one was open for 17% -> 0% of each run, Pallas kernels for 0% -> 25%
where the time goes in v1:
time: 79 us; the launch traced here: 78.7 us
  blocking collectives  35 us (44%)
  Pallas kernels  19.9 us (25%)
  starting transfers between devices  8.49 us (11%)
  waiting for transfers between devices  6.2 us (8%)
  matrix products  5.73 us (7%)
  local copies, waits for them, and re-layouts  3.14 us (4%)
    all_to_all x1, blocking collectives, per_device(): parts = lax.all_to_all(sums, AXES, split_axis=0, concat_axis=0, tiled=True)  20.3 us
    pallas_call x1, Pallas kernels, experts_sums(): pl.pallas_call(functools.partial(experts_kernel, devices), out_shape=jax....  19.9 us
    all_to_all x1, blocking collectives, per_device(): lax.all_to_all(copies, AXES, split_axis=0, concat_axis=0, tiled=True)  14.7 us
    all_to_all x1, starting transfers between devices, per_device(): lax.all_to_all(component_basis, 'ey', split_axis=1, concat_axis=0, tiled=...  8.49 us
    all_to_all x1, waiting for transfers between devices, per_device(): lax.all_to_all(component_basis, 'ey', split_axis=1, concat_axis=0, tiled=...  6.2 us
    dot_general x1, matrix products, per_device(): jnp.dot(weights, relaid, preferred_element_type=jnp.float32)  5.73 us
    all_to_all x1, local copies, waits for them, and re-layouts, per_device(): lax.all_to_all(component_basis, 'ey', split_axis=1, concat_axis=0, tiled=...  3.09 us
  transfers between devices with their start and end apart: 1, of which 1 were waited for; matrix products, arithmetic and copies ran while one was open for 0% of the time, Pallas kernels for 25%

profile of v1, /device:TPU:1, one launch (start us, length us, event | category | flops | bytes accessed | tf_op | source)
XLA Modules:
  0.0 78.7 jit_solution(13515167752070531608)
XLA Ops:
  0.0 3.1 %copy.14 = bf16[2,8,8,8192]{3,2,0,1:T(8,128)(2,1)} copy(bf16[2,8,8,8192]{3,2,1,0:T(8,128)(2,1)} %bitcast.16) | data formatting | bytes 4194304 | tf_op jit(solution)/shard_map/all_to_all | solution.py:215
  3.1 8.5 %all-to-all-start = ((bf16[16,8,8192]{2,0,1:T(8,128)(2,1)}), bf16[16,8,8192]{2,0,1:T(8,128)(2,1)S(1)}, u32[]{:S(2)}, u32[]{:S(2)}) async-start(bf16[16,8,8192]{2,0,1:T(8,128)(2,1)} %bitcast.14), calls=%async_computation | async-start | bytes 4194304 | tf_op jit(solution)/shard_map/all_to_all | solution.py:215
  11.6 0.0 copy-start
  11.6 19.9 %shard_map.91 = f32[64,2,8,128]{3,2,1,0:T(8,128)} custom-call(f32[16,512]{1,0:T(8,128)} %bitcast.19, f32[16,2048]{1,0:T(8,128)} %frequencies_hbm.1, f32[1,2048]{1,0:T(1,128)} %bitcast.20, f32[1,128]{1,0:T(1,128)} %bitcast.21, f32[1,128]{1,0:T(1,128)} %bitcast.22, bf16[2,2048,2048]{2,1,0:T(8,128)(2,1)} %factor_hbm.1, bf16[2,2048,128]{2,1,0:T(8,128)(2,1)} %mean_hbm.1), custom_call_target="tpu_custom_call" | custom-call | flops 9126805504 | bytes 17825792 | tf_op jit(solution)/shard_map/pallas_call | solution.py:166
  31.5 6.2 %all-to-all-done = bf16[16,8,8192]{2,0,1:T(8,128)(2,1)S(1)} async-done(((bf16[16,8,8192]{2,0,1:T(8,128)(2,1)}), bf16[16,8,8192]{2,0,1:T(8,128)(2,1)S(1)}, u32[]{:S(2)}, u32[]{:S(2)}) %all-to-all-start) | async-done | bytes 2097184 | tf_op jit(solution)/shard_map/all_to_all | solution.py:215
  37.7 20.3 %all_to_all.29 = f32[128,8,128]{2,1,0:T(8,128)S(1)} all-to-all(f32[128,8,128]{2,1,0:T(8,128)} %bitcast.17), channel_id=1, replica_groups=mesh['ex'=16,'ey'=8] {'ex','ey'}, dimensions={0} | all-to-all | bytes 1048576 | tf_op jit(solution)/shard_map/all_to_all | solution.py:220
  58.1 0.1 reduce_sum.9
  58.3 14.7 %all_to_all.30 = bf16[128,4,128]{2,1,0:T(4,128)(2,1)S(1)} all-to-all(bf16[128,4,128]{2,1,0:T(4,128)(2,1)S(1)} %broadcast_in_dim.19), channel_id=1, replica_groups=mesh['ex'=16,'ey'=8] {'ex','ey'}, dimensions={0} | all-to-all | bytes 262144 | tf_op jit(solution)/shard_map/all_to_all | solution.py:224
  73.0 0.0 copy-done
  73.0 5.7 %add_convert_fusion = bf16[512,8192]{1,0:T(8,128)(2,1)} fusion(bf16[512,128]{1,0:T(8,128)(2,1)S(1)} %bitcast.18, bf16[128,8192]{1,0:T(8,128)(2,1)S(1)} %bitcast.15, f32[8192]{0:T(1024)S(1)} %copy-done), kind=kOutput, calls=%fused_computation | convolution fusion | flops 1082130432 | bytes 10649600 | tf_op jit(solution)/shard_map/dot_general | solution.py:226
  (2 shorter events, 0.0 us)
Async XLA Ops:
  3.1 34.6 %all-to-all-start = ((bf16[16,8,8192]{2,0,1:T(8,128)(2,1)}), bf16[16,8,8192]{2,0,1:T(8,128)(2,1)S(1)}, u32[]{:S(2)}, u32[]{:S(2)}) async-start(bf16[16,8,8192]{2,0,1:T(8,128)(2,1)} %bitcast.14), calls=%async_computation | async-start | bytes 4194304 | tf_op jit(solution)/shard_map/all_to_all | solution.py:215
  11.6 61.4 %copy-start = (f32[8192]{0:T(1024)S(1)}, f32[8192]{0:T(1024)}, u32[]{:S(2)}) copy-start(f32[8192]{0:T(1024)} %param.17) | copy-start | bytes 98308

commit v2 on v1

--- a/solution.py
+++ b/solution.py
@@ -7,9 +7,13 @@
 from jax import lax
 from jax.experimental import pallas as pl
 from jax.experimental.pallas import tpu as pltpu
+from jax.sharding import Mesh
 from jax.sharding import PartitionSpec as P
 
-AXES = ("ex", "ey")
+EX = ("y_lo", "x", "core")
+EY = ("y_hi", "z")
+AXES = EX + EY
+PLANE = ("y_lo", "y_hi", "z")
 COLUMNS = 512
 ROWS = 32
 LANES = 128
@@ -34,43 +38,26 @@
 
 def experts_kernel(
     devices,
-    settings_hbm,
-    frequencies_hbm,
-    phases_hbm,
-    noise_hbm,
-    scale_hbm,
-    factor_hbm,
-    mean_hbm,
-    out_ref,
     settings,
     frequencies,
     phases,
     noise,
     scale,
+    factor_hbm,
+    mean_hbm,
+    keep_ref,
+    send_ref,
     factor,
     means,
     phi,
     argument,
     squares,
-    small_sems,
+    sums,
     sems,
 ):
     experts, feats, _ = factor.shape
     rows = phi.shape[0]
     chunks = feats // COLUMNS
-    small = [
-        pltpu.make_async_copy(source, target, small_sems.at[i])
-        for i, (source, target) in enumerate(
-            (
-                (settings_hbm, settings),
-                (frequencies_hbm, frequencies),
-                (phases_hbm, phases),
-                (noise_hbm, noise),
-                (scale_hbm, scale),
-                (mean_hbm, means),
-            )
-        )
-    ]
     large = [
         pltpu.make_async_copy(
             factor_hbm.at[e, :, pl.ds(n * COLUMNS, COLUMNS)],
@@ -80,10 +67,9 @@
         for e in range(experts)
         for n in range(chunks)
     ]
-    for copy in small[:5] + large + small[5:]:
+    mean_copy = pltpu.make_async_copy(mean_hbm, means, sems.at[experts * chunks])
+    for copy in large + [mean_copy]:
         copy.start()
-    for copy in small[:5]:
-        copy.wait()
 
     turn = 1.0 / (2.0 * math.pi)
     a0, a1, a2 = split(settings[...])
@@ -133,7 +119,7 @@
             for j in range(1, COLUMNS // LANES):
                 total = total + projected[:, j * LANES : (j + 1) * LANES]
             squares[e] = total if n == 0 else squares[e] + total
-    small[5].wait()
+    mean_copy.wait()
 
     low_half = lax.broadcasted_iota(jnp.int32, (1, 8, LANES), 1) < 4
     step = 128
@@ -154,35 +140,37 @@
         numer = numer.reshape(step // 8, 8, LANES)
         denom = denom.reshape(step // 8, 8, LANES)
         tiles = slice(m * step // 8, (m + 1) * step // 8)
-        out_ref[tiles, 0] = jnp.where(low_half, numer, pltpu.roll(denom, 4, 1))
-        out_ref[tiles, 1] = jnp.where(low_half, pltpu.roll(numer, 4, 1), denom)
+        sums[tiles, 0] = jnp.where(low_half, numer, pltpu.roll(denom, 4, 1))
+        sums[tiles, 1] = jnp.where(low_half, pltpu.roll(numer, 4, 1), denom)
+
+    core = lax.axis_index("core")
+    for g in range(rows // 64):
+        for half in range(2):
+            keep_ref[g, 2 * half : 2 * half + 2] = sums[pl.ds(8 * g + 4 * core + 2 * half, 2)]
+            send_ref[g, 2 * half : 2 * half + 2] = sums[pl.ds(8 * g + 4 * (1 - core) + 2 * half, 2)]
 
 
 def experts_sums(devices, settings, frequencies, phases, noise_var, signal_scale, cov_factor, post_mean):
     experts, feats, _ = cov_factor.shape
-    rows, params = settings.shape
+    rows = settings.shape[0]
     comps = noise_var.shape[0]
     f32, bf16 = jnp.float32, jnp.bfloat16
-    sums = pl.pallas_call(
+    half = jax.ShapeDtypeStruct((rows // 64, 4, 2, 8, comps), f32)
+    return pl.pallas_call(
         functools.partial(experts_kernel, devices),
-        out_shape=jax.ShapeDtypeStruct((rows // 8, 2, 8, comps), f32),
-        in_specs=[pl.BlockSpec(memory_space=pltpu.HBM)] * 7,
-        out_specs=pl.BlockSpec(memory_space=pltpu.VMEM),
+        out_shape=(half, half),
+        in_specs=[pl.BlockSpec(memory_space=pltpu.VMEM)] * 5 + [pl.BlockSpec(memory_space=pltpu.HBM)] * 2,
+        out_specs=(pl.BlockSpec(memory_space=pltpu.VMEM),) * 2,
         scratch_shapes=[
-            pltpu.VMEM((params, rows), f32),
-            pltpu.VMEM((params, feats), f32),
-            pltpu.VMEM((1, feats), f32),
-            pltpu.VMEM((1, comps), f32),
-            pltpu.VMEM((1, comps), f32),
             pltpu.VMEM((experts, feats, feats), bf16),
             pltpu.VMEM((experts, feats, comps), bf16),
             pltpu.VMEM((rows, feats), bf16),
             pltpu.VMEM((rows, feats), f32),
             pltpu.VMEM((experts + 1, rows, comps), f32),
-            pltpu.SemaphoreType.DMA((6,)),
-            pltpu.SemaphoreType.DMA((experts * (feats // COLUMNS),)),
+            pltpu.VMEM((rows // 8, 2, 8, comps), f32),
+            pltpu.SemaphoreType.DMA((experts * (feats // COLUMNS) + 1,)),
         ],
-        compiler_params=pltpu.CompilerParams(vmem_limit_bytes=60 * 2**20),
+        compiler_params=pltpu.CompilerParams(vmem_limit_bytes=48 * 2**20),
         cost_estimate=pl.CostEstimate(
             flops=2 * experts * rows * feats * (feats + comps),
             bytes_accessed=2 * experts * feats * (feats + comps),
@@ -197,7 +185,28 @@
         cov_factor,
         post_mean,
     )
-    return sums.reshape(rows // 4, 8, comps)
+
+
+def combine_kernel(keep_ref, got_ref, *refs):
+    outs, total = refs[:-1], refs[-1]
+    total[...] = keep_ref[...] + got_ref[...]
+    x = lax.axis_index("x")
+    for mask, out_ref in enumerate(outs):
+        for y in range(2):
+            out_ref[y] = total[4 * y + jnp.bitwise_xor(x, mask)]
+
+
+def combine(keep, got):
+    part = jax.ShapeDtypeStruct((2,) + keep.shape[1:], keep.dtype)
+    vmem = pl.BlockSpec(memory_space=pltpu.VMEM)
+    return pl.pallas_call(
+        combine_kernel,
+        out_shape=(part,) * 4,
+        in_specs=[vmem] * 2,
+        out_specs=(vmem,) * 4,
+        scratch_shapes=[pltpu.VMEM(keep.shape, keep.dtype)],
+        compiler_params=pltpu.CompilerParams(vmem_limit_bytes=8 * 2**20),
+    )(keep, got)
 
 
 def per_device(
@@ -212,12 +221,17 @@
     component_basis,
     mean_field,
 ):
-    relaid = lax.all_to_all(component_basis, "ey", split_axis=1, concat_axis=0, tiled=True)
-    sums = experts_sums(
+    relaid = lax.all_to_all(component_basis, EY, split_axis=1, concat_axis=0, tiled=True)
+    keep, send = experts_sums(
         devices, settings, frequencies, phases, noise_var, signal_scale, cov_factor, post_mean
     )
-    relaid, sums = lax.optimization_barrier((relaid, sums))
-    parts = lax.all_to_all(sums, AXES, split_axis=0, concat_axis=0, tiled=True)
+    got = lax.ppermute(send, "core", [(0, 1), (1, 0)])
+    mine, *sends = combine(keep, got)
+    for mask, part in enumerate(sends, 1):
+        mine = mine + lax.ppermute(part, "x", [(i, i ^ mask) for i in range(4)])
+    mine = mine.reshape(16, 8, mine.shape[-1])
+    relaid, mine = lax.optimization_barrier((relaid, mine))
+    parts = lax.all_to_all(mine, PLANE, split_axis=0, concat_axis=0, tiled=True)
     total = jnp.sum(parts, axis=0)
     mine = (total[:4] / total[4:]).astype(jnp.bfloat16)
     copies = jnp.broadcast_to(mine[None], (devices,) + mine.shape)
@@ -236,13 +250,14 @@
         P(),
         P(AXES, None, None),
         P(AXES, None, None),
-        P("ey", "ex"),
+        P(EY, EX),
         P(AXES),
     )
     out_specs = P(None, AXES)
+    fine = Mesh(np.asarray(mesh.devices).reshape(2, 4, 2, 2, 4), AXES)
     return jax.shard_map(
         functools.partial(per_device, mesh.size),
-        mesh=mesh,
+        mesh=fine,
         in_specs=in_specs,
         out_specs=out_specs,
         check_vma=False,

time: 79 us -> 72.3 us (0.915)
  blocking collectives: 35 us -> 28.4 us
  starting transfers between devices: 8.49 us -> 13.5 us
  Pallas kernels: 19.9 us -> 14.9 us
    all_to_all x1, blocking collectives: 20.3 us -> 12.7 us  [per_device(): parts = lax.all_to_all(mine, PLANE, split_axis=0, concat_axis=0, tiled=True)]
    all_to_all x1, waiting for transfers between devices: 6.2 us -> 0.42 us  [per_device(): lax.all_to_all(component_basis, EY, split_axis=1, concat_axis=0, tiled=True)]
    ppermute x0 -> x4, waiting for transfers between devices: none -> 5.73 us  [the longest x3 4.57 us: per_device(): mine = mine + lax.ppermute(part, 'x', [(i, i ^ mask) for i in range(4)])]
    pallas_call x1 -> x2, Pallas kernels: 19.9 us -> 14.9 us  [the longest x1 14.9 us: experts_sums(): pl.pallas_call(functools.partial(experts_kernel, devices), out_shape=(hal...]
    ppermute x0 -> x4, starting transfers between devices: none -> 4.97 us  [the longest x3 3.94 us: per_device(): mine = mine + lax.ppermute(part, 'x', [(i, i ^ mask) for i in range(4)])]
    all_to_all x1, blocking collectives: 14.7 us -> 15.8 us  [per_device(): lax.all_to_all(copies, AXES, split_axis=0, concat_axis=0, tiled=True)]
  transfers between devices with their start and end apart: 1 -> 5, of which waited for: 1 -> 4; matrix products, arithmetic and copies ran while one was open for 0% -> 0% of each run, Pallas kernels for 25% -> 21%
where the time goes in v2:
time: 72.3 us; the launch traced here: 72.1 us
  blocking collectives  28.4 us (39%)
  Pallas kernels  14.9 us (21%)
  starting transfers between devices  13.5 us (19%)
  waiting for transfers between devices  6.15 us (9%)
  matrix products  5.73 us (8%)
  local copies, waits for them, and re-layouts  3.25 us (4%)
    all_to_all x1, blocking collectives, per_device(): lax.all_to_all(copies, AXES, split_axis=0, concat_axis=0, tiled=True)  15.8 us
    pallas_call x1, Pallas kernels, experts_sums(): pl.pallas_call(functools.partial(experts_kernel, devices), out_shape=(hal...  14.9 us
    all_to_all x1, blocking collectives, per_device(): parts = lax.all_to_all(mine, PLANE, split_axis=0, concat_axis=0, tiled=True)  12.7 us
    all_to_all x1, starting transfers between devices, per_device(): lax.all_to_all(component_basis, EY, split_axis=1, concat_axis=0, tiled=True)  8.49 us
    dot_general x1, matrix products, per_device(): jnp.dot(weights, relaid, preferred_element_type=jnp.float32)  5.73 us
    ppermute x3, waiting for transfers between devices, per_device(): mine = mine + lax.ppermute(part, 'x', [(i, i ^ mask) for i in range(4)])  4.57 us
    ppermute x3, starting transfers between devices, per_device(): mine = mine + lax.ppermute(part, 'x', [(i, i ^ mask) for i in range(4)])  3.94 us
    all_to_all x1, local copies, waits for them, and re-layouts, per_device(): lax.all_to_all(component_basis, EY, split_axis=1, concat_axis=0, tiled=True)  3.18 us
  transfers between devices with their start and end apart: 5, of which 4 were waited for; matrix products, arithmetic and copies ran while one was open for 0% of the time, Pallas kernels for 21%

profile of v2, /device:TPU:1, one launch (start us, length us, event | category | flops | bytes accessed | tf_op | source)
XLA Modules:
  0.0 72.1 jit_solution(15166224660407503187)
XLA Ops:
  0.0 0.0 copy-start
  0.0 0.0 copy-start.5
  0.0 0.0 copy-start.4
  0.0 0.0 copy-start.3
  0.0 0.0 copy-start.1
  0.0 0.0 copy-start.2
  0.0 3.2 %copy.14 = bf16[2,8,8,8192]{3,2,0,1:T(8,128)(2,1)} copy(bf16[2,8,8,8192]{3,2,1,0:T(8,128)(2,1)} %bitcast.20) | data formatting | bytes 4194304 | tf_op jit(solution)/shard_map/all_to_all | solution.py:224
  3.2 8.5 %all-to-all-start = ((bf16[16,8,8192]{2,0,1:T(8,128)(2,1)}), bf16[16,8,8192]{2,0,1:T(8,128)(2,1)S(1)}, u32[]{:S(2)}, u32[]{:S(2)}) async-start(bf16[16,8,8192]{2,0,1:T(8,128)(2,1)} %bitcast.14), calls=%async_computation | async-start | bytes 4194304 | tf_op jit(solution)/shard_map/all_to_all | solution.py:224
  11.7 0.0 copy-done
  11.7 0.0 copy-done.5
  11.7 0.0 copy-done.4
  11.7 0.0 copy-done.3
  11.8 0.0 copy-done.1
  11.8 0.0 copy-done.2
  11.8 0.0 copy-start.6
  11.8 14.9 %shard_map.91 = (f32[8,4,2,8,128]{4,3,2,1,0:T(8,128)S(1)}, f32[8,4,2,8,128]{4,3,2,1,0:T(8,128)S(1)}) custom-call(f32[16,512]{1,0:T(8,128)S(1)} %bitcast.15, f32[16,2048]{1,0:T(8,128)S(1)} %copy-done.1, f32[1,2048]{1,0:T(1,128)S(1)} %bitcast.16, f32[1,128]{1,0:T(1,128)S(1)} %bitcast.17, f32[1,128]{1,0:T(1,128)S(1)} %bitcast.18, ...), custom_call_target="tpu_custom_call" | custom-call | flops 9126805504 | bytes 17825792 | tf_op jit(solution)/shard_map/pallas_call | solution.py:159
  26.7 1.0 %collective-permute-start = (f32[8,4,2,8,128]{4,3,2,1,0:T(8,128)S(1)}, f32[8,4,2,8,128]{4,3,2,1,0:T(8,128)S(1)}, u32[]{:S(2)}, u32[]{:S(2)}) collective-permute-start(f32[8,4,2,8,128]{4,3,2,1,0:T(8,128)S(1)} %get-tuple-element.14), channel_id=1, source_target_pairs={{0,8},{8,0},{1,9},{9,1},{2,10},{10,2},{3,11},{11,3},{4,12},{12,4},... | collective-permute-start | bytes 786440 | tf_op jit(solution)/shard_map/ppermute | solution.py:228
  27.7 1.2 %collective-permute-done.got_ref = f32[8,4,2,8,128]{4,3,2,1,0:T(8,128)S(1)} collective-permute-done((f32[8,4,2,8,128]{4,3,2,1,0:T(8,128)S(1)}, f32[8,4,2,8,128]{4,3,2,1,0:T(8,128)S(1)}, u32[]{:S(2)}, u32[]{:S(2)}) %collective-permute-start) | collective-permute-done | bytes 262176 | tf_op jit(solution)/shard_map/ppermute | solution.py:228
  28.9 1.3 %collective-permute-start.1 = (f32[2,4,2,8,128]{4,3,2,1,0:T(8,128)S(1)}, f32[2,4,2,8,128]{4,3,2,1,0:T(8,128)S(1)}, u32[]{:S(2)}, u32[]{:S(2)}) collective-permute-start(f32[2,4,2,8,128]{4,3,2,1,0:T(8,128)S(1)} %get-tuple-element.16), channel_id=1, source_target_pairs={{0,16},{16,0},{32,48},{48,32},{1,17},{17,1},{33,49},{49,33},{2,18}... | collective-permute-start | bytes 196616 | tf_op jit(solution)/shard_map/ppermute | solution.py:231
  30.2 2.5 %collective-permute-start.2 = (f32[2,4,2,8,128]{4,3,2,1,0:T(8,128)S(1)}, f32[2,4,2,8,128]{4,3,2,1,0:T(8,128)S(1)}, u32[]{:S(2)}, u32[]{:S(2)}) collective-permute-start(f32[2,4,2,8,128]{4,3,2,1,0:T(8,128)S(1)} %get-tuple-element.17), channel_id=1, source_target_pairs={{0,32},{16,48},{32,0},{48,16},{1,33},{17,49},{33,1},{49,17},{2,34}... | collective-permute-start | bytes 196616 | tf_op jit(solution)/shard_map/ppermute | solution.py:231
  32.7 0.2 collective-permute-start.3
  32.9 0.0 collective-permute-done.1
  32.9 3.1 %collective-permute-done.2 = f32[2,4,2,8,128]{4,3,2,1,0:T(8,128)S(1)} collective-permute-done((f32[2,4,2,8,128]{4,3,2,1,0:T(8,128)S(1)}, f32[2,4,2,8,128]{4,3,2,1,0:T(8,128)S(1)}, u32[]{:S(2)}, u32[]{:S(2)}) %collective-permute-start.2) | collective-permute-done | bytes 65568 | tf_op jit(solution)/shard_map/ppermute | solution.py:231
  35.9 1.5 %collective-permute-done.3 = f32[2,4,2,8,128]{4,3,2,1,0:T(8,128)S(1)} collective-permute-done((f32[2,4,2,8,128]{4,3,2,1,0:T(8,128)S(1)}, f32[2,4,2,8,128]{4,3,2,1,0:T(8,128)S(1)}, u32[]{:S(2)}, u32[]{:S(2)}) %collective-permute-start.3) | collective-permute-done | bytes 65568 | tf_op jit(solution)/shard_map/ppermute | solution.py:231
  37.4 0.4 all-to-all-done
  37.9 12.7 %all_to_all.29 = f32[16,8,128]{2,1,0:T(8,128)S(1)} all-to-all(f32[16,8,128]{2,1,0:T(8,128)S(1)} %bitcast.22), channel_id=1, replica_groups=mesh['y_lo'=2,'x'=4,'core'=2,'y_hi'=2,'z'=4] {'y_lo','y_hi','z'}, dimensions={0} | all-to-all | bytes 131072 | tf_op jit(solution)/shard_map/all_to_all | solution.py:234
  50.6 15.8 %all_to_all.30 = bf16[128,4,128]{2,1,0:T(4,128)(2,1)S(1)} all-to-all(bf16[128,4,128]{2,1,0:T(4,128)(2,1)S(1)} %broadcast_in_dim.19), channel_id=1, replica_groups=mesh['y_lo'=2,'x'=4,'core'=2,'y_hi'=2,'z'=4] {'y_lo','x','core','y_hi','z'}, dimensions={0} | all-to-all | bytes 262144 | tf_op jit(solution)/shard_map/all_to_all | solution.py:238
  66.4 0.0 copy-done.6
  66.4 5.7 %add_convert_fusion = bf16[512,8192]{1,0:T(8,128)(2,1)} fusion(bf16[512,128]{1,0:T(8,128)(2,1)S(1)} %bitcast.21, bf16[128,8192]{1,0:T(8,128)(2,1)S(1)} %bitcast.19, f32[8192]{0:T(1024)S(1)} %copy-done.6), kind=kOutput, calls=%fused_computation | convolution fusion | flops 1082130432 | bytes 10649600 | tf_op jit(solution)/shard_map/dot_general | solution.py:240
  (5 shorter events, 0.1 us)
Async XLA Ops:
  0.0 11.7 %copy-start = (bf16[2,2048,128]{2,1,0:T(8,128)(2,1)S(1)}, bf16[2,2048,128]{2,1,0:T(8,128)(2,1)}, u32[]{:S(2)}) copy-start(bf16[2,2048,128]{2,1,0:T(8,128)(2,1)} %mean_hbm.1) | copy-start | bytes 3145732
  0.0 11.7 %copy-start.5 = (f32[128]{0:T(128)S(1)}, f32[128]{0:T(128)}, u32[]{:S(2)}) copy-start(f32[128]{0:T(128)} %param.13) | copy-start | bytes 1540
  0.0 11.7 %copy-start.4 = (f32[128]{0:T(128)S(1)}, f32[128]{0:T(128)}, u32[]{:S(2)}) copy-start(f32[128]{0:T(128)} %param.12) | copy-start | bytes 1540
  0.0 11.7 %copy-start.3 = (f32[2048]{0:T(1024)S(1)}, f32[2048]{0:T(1024)}, u32[]{:S(2)}) copy-start(f32[2048]{0:T(1024)} %param.11) | copy-start | bytes 24580
  0.0 11.7 %copy-start.1 = (f32[16,2048]{1,0:T(8,128)S(1)}, f32[16,2048]{1,0:T(8,128)}, u32[]{:S(2)}) copy-start(f32[16,2048]{1,0:T(8,128)} %frequencies.1) | copy-start | bytes 393220
  0.0 11.7 %copy-start.2 = (f32[512,16]{0,1:T(8,128)S(1)}, f32[512,16]{0,1:T(8,128)}, u32[]{:S(2)}) copy-start(f32[512,16]{0,1:T(8,128)} %param.9) | copy-start | bytes 98308
  3.2 34.6 %all-to-all-start = ((bf16[16,8,8192]{2,0,1:T(8,128)(2,1)}), bf16[16,8,8192]{2,0,1:T(8,128)(2,1)S(1)}, u32[]{:S(2)}, u32[]{:S(2)}) async-start(bf16[16,8,8192]{2,0,1:T(8,128)(2,1)} %bitcast.14), calls=%async_computation | async-start | bytes 4194304 | tf_op jit(solution)/shard_map/all_to_all | solution.py:224
  11.8 54.6 %copy-start.6 = (f32[8192]{0:T(1024)S(1)}, f32[8192]{0:T(1024)}, u32[]{:S(2)}) copy-start(f32[8192]{0:T(1024)} %param.17) | copy-start | bytes 98308
  26.7 2.2 %collective-permute-start = (f32[8,4,2,8,128]{4,3,2,1,0:T(8,128)S(1)}, f32[8,4,2,8,128]{4,3,2,1,0:T(8,128)S(1)}, u32[]{:S(2)}, u32[]{:S(2)}) collective-permute-start(f32[8,4,2,8,128]{4,3,2,1,0:T(8,128)S(1)} %get-tuple-element.14), channel_id=1, source_target_pairs={{0,8},{8,0},{1,9},{9,1},{2,10},{10,2},{3,11},{11,3},{4,12},{12,4},... | collective-permute-start | bytes 786440 | tf_op jit(solution)/shard_map/ppermute | solution.py:228
  28.9 3.9 %collective-permute-start.1 = (f32[2,4,2,8,128]{4,3,2,1,0:T(8,128)S(1)}, f32[2,4,2,8,128]{4,3,2,1,0:T(8,128)S(1)}, u32[]{:S(2)}, u32[]{:S(2)}) collective-permute-start(f32[2,4,2,8,128]{4,3,2,1,0:T(8,128)S(1)} %get-tuple-element.16), channel_id=1, source_target_pairs={{0,16},{16,0},{32,48},{48,32},{1,17},{17,1},{33,49},{49,33},{2,18}... | collective-permute-start | bytes 196616 | tf_op jit(solution)/shard_map/ppermute | solution.py:231
  30.2 5.7 %collective-permute-start.2 = (f32[2,4,2,8,128]{4,3,2,1,0:T(8,128)S(1)}, f32[2,4,2,8,128]{4,3,2,1,0:T(8,128)S(1)}, u32[]{:S(2)}, u32[]{:S(2)}) collective-permute-start(f32[2,4,2,8,128]{4,3,2,1,0:T(8,128)S(1)} %get-tuple-element.17), channel_id=1, source_target_pairs={{0,32},{16,48},{32,0},{48,16},{1,33},{17,49},{33,1},{49,17},{2,34}... | collective-permute-start | bytes 196616 | tf_op jit(solution)/shard_map/ppermute | solution.py:231
  32.7 4.8 %collective-permute-start.3 = (f32[2,4,2,8,128]{4,3,2,1,0:T(8,128)S(1)}, f32[2,4,2,8,128]{4,3,2,1,0:T(8,128)S(1)}, u32[]{:S(2)}, u32[]{:S(2)}) collective-permute-start(f32[2,4,2,8,128]{4,3,2,1,0:T(8,128)S(1)} %get-tuple-element.18), channel_id=1, source_target_pairs={{0,48},{16,32},{32,16},{48,0},{1,49},{17,33},{33,17},{49,1},{2,50}... | collective-permute-start | bytes 196616 | tf_op jit(solution)/shard_map/ppermute | solution.py:231

commit v3 on v2

--- a/solution.py
+++ b/solution.py
@@ -14,6 +14,7 @@
 EY = ("y_hi", "z")
 AXES = EX + EY
 PLANE = ("y_lo", "y_hi", "z")
+OWNERS = ("x", "core", "z")
 COLUMNS = 512
 ROWS = 32
 LANES = 128
@@ -121,7 +122,6 @@
             squares[e] = total if n == 0 else squares[e] + total
     mean_copy.wait()
 
-    low_half = lax.broadcasted_iota(jnp.int32, (1, 8, LANES), 1) < 4
     step = 128
     for m in range(rows // step):
         block = slice(m * step, (m + 1) * step)
@@ -137,17 +137,12 @@
             inv_variance = 1.0 / variance
             numer = numer + robust * inv_variance * mean
             denom = denom + robust * (inv_variance - inv_prior)
-        numer = numer.reshape(step // 8, 8, LANES)
-        denom = denom.reshape(step // 8, 8, LANES)
-        tiles = slice(m * step // 8, (m + 1) * step // 8)
-        sums[tiles, 0] = jnp.where(low_half, numer, pltpu.roll(denom, 4, 1))
-        sums[tiles, 1] = jnp.where(low_half, pltpu.roll(numer, 4, 1), denom)
+        sums[m] = jnp.stack([numer.reshape(-1, 16, LANES), denom.reshape(-1, 16, LANES)], axis=1)
 
     core = lax.axis_index("core")
-    for g in range(rows // 64):
-        for half in range(2):
-            keep_ref[g, 2 * half : 2 * half + 2] = sums[pl.ds(8 * g + 4 * core + 2 * half, 2)]
-            send_ref[g, 2 * half : 2 * half + 2] = sums[pl.ds(8 * g + 4 * (1 - core) + 2 * half, 2)]
+    for x in range(4):
+        keep_ref[x] = sums[x, pl.ds(4 * core, 4)]
+        send_ref[x] = sums[x, pl.ds(4 * (1 - core), 4)]
 
 
 def experts_sums(devices, settings, frequencies, phases, noise_var, signal_scale, cov_factor, post_mean):
@@ -155,7 +150,7 @@
     rows = settings.shape[0]
     comps = noise_var.shape[0]
     f32, bf16 = jnp.float32, jnp.bfloat16
-    half = jax.ShapeDtypeStruct((rows // 64, 4, 2, 8, comps), f32)
+    half = jax.ShapeDtypeStruct((4, 4, 2, 16, comps), f32)
     return pl.pallas_call(
         functools.partial(experts_kernel, devices),
         out_shape=(half, half),
@@ -167,7 +162,7 @@
             pltpu.VMEM((rows, feats), bf16),
             pltpu.VMEM((rows, feats), f32),
             pltpu.VMEM((experts + 1, rows, comps), f32),
-            pltpu.VMEM((rows // 8, 2, 8, comps), f32),
+            pltpu.VMEM((4, 8, 2, 16, comps), f32),
             pltpu.SemaphoreType.DMA((experts * (feats // COLUMNS) + 1,)),
         ],
         compiler_params=pltpu.CompilerParams(vmem_limit_bytes=48 * 2**20),
@@ -192,12 +187,11 @@
     total[...] = keep_ref[...] + got_ref[...]
     x = lax.axis_index("x")
     for mask, out_ref in enumerate(outs):
-        for y in range(2):
-            out_ref[y] = total[4 * y + jnp.bitwise_xor(x, mask)]
+        out_ref[...] = total[jnp.bitwise_xor(x, mask)]
 
 
 def combine(keep, got):
-    part = jax.ShapeDtypeStruct((2,) + keep.shape[1:], keep.dtype)
+    part = jax.ShapeDtypeStruct(keep.shape[1:], keep.dtype)
     vmem = pl.BlockSpec(memory_space=pltpu.VMEM)
     return pl.pallas_call(
         combine_kernel,
@@ -207,6 +201,78 @@
         scratch_shapes=[pltpu.VMEM(keep.shape, keep.dtype)],
         compiler_params=pltpu.CompilerParams(vmem_limit_bytes=8 * 2**20),
     )(keep, got)
+
+
+def relay_kernel(basis, out_ref, held, read_sems, write_sems):
+    devices, _, cells = out_ref.shape
+    reads = [
+        pltpu.make_async_copy(basis.at[:, pl.ds(d * cells, cells)], held.at[d], read_sems.at[d])
+        for d in range(devices)
+    ]
+    writes = [
+        pltpu.make_async_copy(held.at[d], out_ref.at[d], write_sems.at[d]) for d in range(devices)
+    ]
+    for copy in reads:
+        copy.start()
+    for read, write in zip(reads, writes):
+        read.wait()
+        write.start()
+    for copy in writes:
+        copy.wait()
+
+
+def relay(basis, devices):
+    comps, cells = basis.shape
+    shape = (devices, comps, cells // devices)
+    return pl.pallas_call(
+        relay_kernel,
+        out_shape=jax.ShapeDtypeStruct(shape, basis.dtype),
+        in_specs=[pl.BlockSpec(memory_space=pltpu.HBM)],
+        out_specs=pl.BlockSpec(memory_space=pltpu.HBM),
+        scratch_shapes=[
+            pltpu.VMEM(shape, basis.dtype),
+            pltpu.SemaphoreType.DMA((devices,)),
+            pltpu.SemaphoreType.DMA((devices,)),
+        ],
+        compiler_params=pltpu.CompilerParams(vmem_limit_bytes=60 * 2**20),
+    )(basis)
+
+
+def stock_kernel(weights, basis, mean, out_ref, stock, sems):
+    chunks = sems.shape[0]
+    cells = basis.shape[1] // chunks
+    copies = []
+    for c in range(chunks):
+        for n in range(cells // 256):
+            span = slice(c * cells + n * 256, c * cells + (n + 1) * 256)
+            tile = jnp.dot(weights[...], basis[:, span], preferred_element_type=jnp.float32)
+            stock[:, span] = (tile + mean[:, span]).astype(jnp.bfloat16)
+        span = pl.ds(c * cells, cells)
+        copies.append(pltpu.make_async_copy(stock.at[:, span], out_ref.at[:, span], sems.at[c]))
+        copies[-1].start()
+    for copy in copies:
+        copy.wait()
+
+
+def stock_of(weights, basis, mean_field):
+    rows, comps = weights.shape
+    cells = mean_field.shape[0]
+    chunks = 16
+    vmem = pl.BlockSpec(memory_space=pltpu.VMEM)
+    return pl.pallas_call(
+        stock_kernel,
+        out_shape=jax.ShapeDtypeStruct((rows, cells), jnp.bfloat16),
+        in_specs=[vmem] * 3,
+        out_specs=pl.BlockSpec(memory_space=pltpu.HBM),
+        scratch_shapes=[
+            pltpu.VMEM((rows, cells), jnp.bfloat16),
+            pltpu.SemaphoreType.DMA((chunks,)),
+        ],
+        compiler_params=pltpu.CompilerParams(vmem_limit_bytes=24 * 2**20),
+        cost_estimate=pl.CostEstimate(
+            flops=2 * rows * comps * cells, bytes_accessed=2 * rows * cells, transcendentals=0
+        ),
+    )(weights, basis, mean_field[None, :])
 
 
 def per_device(
@@ -221,7 +287,8 @@
     component_basis,
     mean_field,
 ):
-    relaid = lax.all_to_all(component_basis, EY, split_axis=1, concat_axis=0, tiled=True)
+    relaid = lax.all_to_all(relay(component_basis, 8), EY, split_axis=0, concat_axis=0, tiled=True)
+    relaid = relaid.reshape(-1, relaid.shape[-1])
     keep, send = experts_sums(
         devices, settings, frequencies, phases, noise_var, signal_scale, cov_factor, post_mean
     )
@@ -229,16 +296,14 @@
     mine, *sends = combine(keep, got)
     for mask, part in enumerate(sends, 1):
         mine = mine + lax.ppermute(part, "x", [(i, i ^ mask) for i in range(4)])
-    mine = mine.reshape(16, 8, mine.shape[-1])
     relaid, mine = lax.optimization_barrier((relaid, mine))
+    mine = jnp.broadcast_to(mine[None], (4,) + mine.shape).reshape((16,) + mine.shape[1:])
     parts = lax.all_to_all(mine, PLANE, split_axis=0, concat_axis=0, tiled=True)
-    total = jnp.sum(parts, axis=0)
-    mine = (total[:4] / total[4:]).astype(jnp.bfloat16)
-    copies = jnp.broadcast_to(mine[None], (devices,) + mine.shape)
-    weights = lax.all_to_all(copies, AXES, split_axis=0, concat_axis=0, tiled=True)
-    weights = weights.reshape(settings.shape[0], noise_var.shape[0])
-    stock = jnp.dot(weights, relaid, preferred_element_type=jnp.float32) + mean_field[None, :]
-    return stock.astype(jnp.bfloat16)
+    numer, denom = jnp.sum(parts, axis=0)
+    mine = (numer / denom).astype(jnp.bfloat16)
+    copies = jnp.broadcast_to(mine[None], (32,) + mine.shape)
+    weights = lax.all_to_all(copies, OWNERS, split_axis=0, concat_axis=0, tiled=True)
+    return stock_of(weights.reshape(settings.shape[0], -1), relaid, mean_field)
 
 
 def solution(mesh):

time: 72.3 us -> 69 us (0.954)
  Pallas kernels: 14.9 us -> 21 us
  matrix products: 5.73 us -> 0 us
  local copies, waits for them, and re-layouts: 3.25 us -> 0.08 us
  blocking collectives: 28.4 us -> 27.5 us
    pallas_call x0 -> x2, Pallas kernels: none -> 6.09 us  [the longest x1 3.7 us: stock_of(): pl.pallas_call(stock_kernel, out_shape=jax.ShapeDtypeStruct((rows, cells)...]
    dot_general x1 -> x0, matrix products: 5.73 us -> none  [per_device(): jnp.dot(weights, relaid, preferred_element_type=jnp.float32)]
    all_to_all x1 -> x0, local copies, waits for them, and re-layouts: 3.18 us -> none  [per_device(): lax.all_to_all(component_basis, EY, split_axis=1, concat_axis=0, tiled=True)]
    all_to_all x1, blocking collectives: 15.8 us -> 14 us  [per_device(): lax.all_to_all(copies, OWNERS, split_axis=0, concat_axis=0, tiled=True)]
    all_to_all x1, blocking collectives: 12.7 us -> 13.4 us  [per_device(): parts = lax.all_to_all(mine, PLANE, split_axis=0, concat_axis=0, tiled=True)]
  transfers between devices with their start and end apart: 5 -> 5, of which waited for: 4 -> 4; matrix products, arithmetic and copies ran while one was open for 0% -> 0% of each run, Pallas kernels for 21% -> 22%
where the time goes in v3:
time: 69 us; the launch traced here: 68.7 us
  blocking collectives  27.5 us (40%)
  Pallas kernels  21 us (30%)
  starting transfers between devices  13.6 us (20%)
  waiting for transfers between devices  6.2 us (9%)
    pallas_call x1, Pallas kernels, experts_sums(): pl.pallas_call(functools.partial(experts_kernel, devices), out_shape=(hal...  14.8 us
    all_to_all x1, blocking collectives, per_device(): lax.all_to_all(copies, OWNERS, split_axis=0, concat_axis=0, tiled=True)  14 us
    all_to_all x1, blocking collectives, per_device(): parts = lax.all_to_all(mine, PLANE, split_axis=0, concat_axis=0, tiled=True)  13.4 us
    all_to_all x1, starting transfers between devices, per_device(): lax.all_to_all(relay(component_basis, 8), EY, split_axis=0, concat_axis=0...  8.64 us
    ppermute x3, waiting for transfers between devices, per_device(): mine = mine + lax.ppermute(part, 'x', [(i, i ^ mask) for i in range(4)])  4.56 us
    ppermute x3, starting transfers between devices, per_device(): mine = mine + lax.ppermute(part, 'x', [(i, i ^ mask) for i in range(4)])  3.94 us
    pallas_call x1, Pallas kernels, stock_of(): pl.pallas_call(stock_kernel, out_shape=jax.ShapeDtypeStruct((rows, cells)...  3.7 us
    pallas_call x1, Pallas kernels, relay(): pl.pallas_call(relay_kernel, out_shape=jax.ShapeDtypeStruct(shape, basis....  2.39 us
  transfers between devices with their start and end apart: 5, of which 4 were waited for; matrix products, arithmetic and copies ran while one was open for 0% of the time, Pallas kernels for 22%

profile of v3, /device:TPU:1, one launch (start us, length us, event | category | flops | bytes accessed | tf_op | source)
XLA Modules:
  0.0 68.7 jit_solution(472543039843217264)
XLA Ops:
  0.0 2.4 %shard_map.91 = bf16[8,16,8192]{2,1,0:T(8,128)(2,1)} custom-call(bf16[16,65536]{1,0:T(8,128)(2,1)} %basis.1), custom_call_target="tpu_custom_call" | custom-call | tf_op jit(solution)/shard_map/pallas_call | solution.py:227
  2.4 0.0 copy-start.1
  2.4 0.0 copy-start.2
  2.4 0.0 copy-start.3
  2.4 0.0 copy-start.4
  2.4 0.0 copy-start.5
  2.5 0.0 copy-start.6
  2.5 8.6 %all-to-all-start = ((bf16[8,16,8192]{2,1,0:T(8,128)(2,1)}), bf16[8,16,8192]{2,1,0:T(8,128)(2,1)S(1)}, u32[]{:S(2)}, u32[]{:S(2)}) async-start(bf16[8,16,8192]{2,1,0:T(8,128)(2,1)} %shard_map.91), calls=%async_computation | async-start | bytes 4194304 | tf_op jit(solution)/shard_map/all_to_all | solution.py:290
  11.1 0.0 copy-done.1
  11.1 0.0 copy-done.2
  11.1 0.0 copy-done.3
  11.1 0.0 copy-done.4
  11.1 0.0 copy-done.5
  11.2 0.0 copy-done.6
  11.2 14.8 %shard_map.92 = (f32[4,4,2,16,128]{4,3,2,1,0:T(8,128)S(1)}, f32[4,4,2,16,128]{4,3,2,1,0:T(8,128)S(1)}) custom-call(f32[16,512]{1,0:T(8,128)S(1)} %bitcast.13, f32[16,2048]{1,0:T(8,128)S(1)} %copy-done.2, f32[1,2048]{1,0:T(1,128)S(1)} %bitcast.14, f32[1,128]{1,0:T(1,128)S(1)} %bitcast.15, f32[1,128]{1,0:T(1,128)S(1)} %bitcast.16, ...), custom_call_target="tpu_custom_call" | custom-call | flops 9126805504 | bytes 17825792 | tf_op jit(solution)/shard_map/pallas_call | solution.py:154
  26.0 0.0 copy-start
  26.0 1.0 %collective-permute-start = (f32[4,4,2,16,128]{4,3,2,1,0:T(8,128)S(1)}, f32[4,4,2,16,128]{4,3,2,1,0:T(8,128)S(1)}, u32[]{:S(2)}, u32[]{:S(2)}) collective-permute-start(f32[4,4,2,16,128]{4,3,2,1,0:T(8,128)S(1)} %get-tuple-element.14), channel_id=1, source_target_pairs={{0,8},{8,0},{1,9},{9,1},{2,10},{10,2},{3,11},{11,3},{4,12},{12,4},... | collective-permute-start | bytes 786440 | tf_op jit(solution)/shard_map/ppermute | solution.py:295
  27.0 1.2 %collective-permute-done.got_ref = f32[4,4,2,16,128]{4,3,2,1,0:T(8,128)S(1)} collective-permute-done((f32[4,4,2,16,128]{4,3,2,1,0:T(8,128)S(1)}, f32[4,4,2,16,128]{4,3,2,1,0:T(8,128)S(1)}, u32[]{:S(2)}, u32[]{:S(2)}) %collective-permute-start) | collective-permute-done | bytes 262176 | tf_op jit(solution)/shard_map/ppermute | solution.py:295
  28.3 1.3 %collective-permute-start.1 = (f32[4,2,16,128]{3,2,1,0:T(8,128)S(1)}, f32[4,2,16,128]{3,2,1,0:T(8,128)S(1)}, u32[]{:S(2)}, u32[]{:S(2)}) collective-permute-start(f32[4,2,16,128]{3,2,1,0:T(8,128)S(1)} %get-tuple-element.16), channel_id=1, source_target_pairs={{0,16},{16,0},{32,48},{48,32},{1,17},{17,1},{33,49},{49,33},{2,18}... | collective-permute-start | bytes 196616 | tf_op jit(solution)/shard_map/ppermute | solution.py:298
  29.5 2.5 %collective-permute-start.2 = (f32[4,2,16,128]{3,2,1,0:T(8,128)S(1)}, f32[4,2,16,128]{3,2,1,0:T(8,128)S(1)}, u32[]{:S(2)}, u32[]{:S(2)}) collective-permute-start(f32[4,2,16,128]{3,2,1,0:T(8,128)S(1)} %get-tuple-element.17), channel_id=1, source_target_pairs={{0,32},{16,48},{32,0},{48,16},{1,33},{17,49},{33,1},{49,17},{2,34}... | collective-permute-start | bytes 196616 | tf_op jit(solution)/shard_map/ppermute | solution.py:298
  32.0 0.2 collective-permute-start.3
  32.2 0.0 collective-permute-done.1
  32.2 3.0 %collective-permute-done.2 = f32[4,2,16,128]{3,2,1,0:T(8,128)S(1)} collective-permute-done((f32[4,2,16,128]{3,2,1,0:T(8,128)S(1)}, f32[4,2,16,128]{3,2,1,0:T(8,128)S(1)}, u32[]{:S(2)}, u32[]{:S(2)}) %collective-permute-start.2) | collective-permute-done | bytes 65568 | tf_op jit(solution)/shard_map/ppermute | solution.py:298
  35.2 1.5 %collective-permute-done.3 = f32[4,2,16,128]{3,2,1,0:T(8,128)S(1)} collective-permute-done((f32[4,2,16,128]{3,2,1,0:T(8,128)S(1)}, f32[4,2,16,128]{3,2,1,0:T(8,128)S(1)}, u32[]{:S(2)}, u32[]{:S(2)}) %collective-permute-start.3) | collective-permute-done | bytes 65568 | tf_op jit(solution)/shard_map/ppermute | solution.py:298
  36.8 0.5 all-to-all-done
  37.3 13.4 %all_to_all.15 = f32[16,2,16,128]{3,2,1,0:T(8,128)S(1)} all-to-all(f32[16,2,16,128]{3,2,1,0:T(8,128)S(1)} %bitcast.17), channel_id=1, replica_groups=mesh['y_lo'=2,'x'=4,'core'=2,'y_hi'=2,'z'=4] {'y_lo','y_hi','z'}, dimensions={0} | all-to-all | bytes 524288 | tf_op jit(solution)/shard_map/all_to_all | solution.py:301
  50.8 14.0 %all_to_all.16 = bf16[32,16,128]{2,1,0:T(8,128)(2,1)S(1)} all-to-all(bf16[32,16,128]{2,1,0:T(8,128)(2,1)S(1)} %broadcast_in_dim.31), channel_id=1, replica_groups=mesh['y_lo'=2,'x'=4,'core'=2,'y_hi'=2,'z'=4] {'x','core','z'}, dimensions={0} | all-to-all | bytes 262144 | tf_op jit(solution)/shard_map/all_to_all | solution.py:305
  64.8 0.0 copy-done
  64.8 3.7 %shard_map.94 = bf16[512,8192]{1,0:T(8,128)(2,1)} custom-call(bf16[512,128]{1,0:T(8,128)(2,1)S(1)} %bitcast.11, bf16[128,8192]{1,0:T(8,128)(2,1)S(1)} %bitcast.10, f32[1,8192]{1,0:T(1,128)S(1)} %bitcast.12), custom_call_target="tpu_custom_call" | custom-call | flops 1073741824 | bytes 8388608 | tf_op jit(solution)/shard_map/pallas_call | solution.py:262
  (6 shorter events, 0.1 us)
Async XLA Ops:
  2.4 8.7 %copy-start.1 = (bf16[2,2048,128]{2,1,0:T(8,128)(2,1)S(1)}, bf16[2,2048,128]{2,1,0:T(8,128)(2,1)}, u32[]{:S(2)}) copy-start(bf16[2,2048,128]{2,1,0:T(8,128)(2,1)} %mean_hbm.1) | copy-start | bytes 3145732
  2.4 8.7 %copy-start.2 = (f32[16,2048]{1,0:T(8,128)S(1)}, f32[16,2048]{1,0:T(8,128)}, u32[]{:S(2)}) copy-start(f32[16,2048]{1,0:T(8,128)} %frequencies.1) | copy-start | bytes 393220
  2.4 8.7 %copy-start.3 = (f32[512,16]{0,1:T(8,128)S(1)}, f32[512,16]{0,1:T(8,128)}, u32[]{:S(2)}) copy-start(f32[512,16]{0,1:T(8,128)} %param.9) | copy-start | bytes 98308
  2.4 8.7 %copy-start.4 = (f32[2048]{0:T(1024)S(1)}, f32[2048]{0:T(1024)}, u32[]{:S(2)}) copy-start(f32[2048]{0:T(1024)} %param.11) | copy-start | bytes 24580
  2.4 8.7 %copy-start.5 = (f32[128]{0:T(128)S(1)}, f32[128]{0:T(128)}, u32[]{:S(2)}) copy-start(f32[128]{0:T(128)} %param.12) | copy-start | bytes 1540
  2.5 8.7 %copy-start.6 = (f32[128]{0:T(128)S(1)}, f32[128]{0:T(128)}, u32[]{:S(2)}) copy-start(f32[128]{0:T(128)} %param.13) | copy-start | bytes 1540
  2.5 34.8 %all-to-all-start = ((bf16[8,16,8192]{2,1,0:T(8,128)(2,1)}), bf16[8,16,8192]{2,1,0:T(8,128)(2,1)S(1)}, u32[]{:S(2)}, u32[]{:S(2)}) async-start(bf16[8,16,8192]{2,1,0:T(8,128)(2,1)} %shard_map.91), calls=%async_computation | async-start | bytes 4194304 | tf_op jit(solution)/shard_map/all_to_all | solution.py:290
  26.0 38.8 %copy-start = (f32[8192]{0:T(1024)S(1)}, f32[8192]{0:T(1024)}, u32[]{:S(2)}) copy-start(f32[8192]{0:T(1024)} %param.17) | copy-start | bytes 98308
  26.0 2.2 %collective-permute-start = (f32[4,4,2,16,128]{4,3,2,1,0:T(8,128)S(1)}, f32[4,4,2,16,128]{4,3,2,1,0:T(8,128)S(1)}, u32[]{:S(2)}, u32[]{:S(2)}) collective-permute-start(f32[4,4,2,16,128]{4,3,2,1,0:T(8,128)S(1)} %get-tuple-element.14), channel_id=1, source_target_pairs={{0,8},{8,0},{1,9},{9,1},{2,10},{10,2},{3,11},{11,3},{4,12},{12,4},... | collective-permute-start | bytes 786440 | tf_op jit(solution)/shard_map/ppermute | solution.py:295
  28.3 3.9 %collective-permute-start.1 = (f32[4,2,16,128]{3,2,1,0:T(8,128)S(1)}, f32[4,2,16,128]{3,2,1,0:T(8,128)S(1)}, u32[]{:S(2)}, u32[]{:S(2)}) collective-permute-start(f32[4,2,16,128]{3,2,1,0:T(8,128)S(1)} %get-tuple-element.16), channel_id=1, source_target_pairs={{0,16},{16,0},{32,48},{48,32},{1,17},{17,1},{33,49},{49,33},{2,18}... | collective-permute-start | bytes 196616 | tf_op jit(solution)/shard_map/ppermute | solution.py:298
  29.5 5.7 %collective-permute-start.2 = (f32[4,2,16,128]{3,2,1,0:T(8,128)S(1)}, f32[4,2,16,128]{3,2,1,0:T(8,128)S(1)}, u32[]{:S(2)}, u32[]{:S(2)}) collective-permute-start(f32[4,2,16,128]{3,2,1,0:T(8,128)S(1)} %get-tuple-element.17), channel_id=1, source_target_pairs={{0,32},{16,48},{32,0},{48,16},{1,33},{17,49},{33,1},{49,17},{2,34}... | collective-permute-start | bytes 196616 | tf_op jit(solution)/shard_map/ppermute | solution.py:298
  32.0 4.8 %collective-permute-start.3 = (f32[4,2,16,128]{3,2,1,0:T(8,128)S(1)}, f32[4,2,16,128]{3,2,1,0:T(8,128)S(1)}, u32[]{:S(2)}, u32[]{:S(2)}) collective-permute-start(f32[4,2,16,128]{3,2,1,0:T(8,128)S(1)} %get-tuple-element.18), channel_id=1, source_target_pairs={{0,48},{16,32},{32,16},{48,0},{1,49},{17,33},{33,17},{49,1},{2,50}... | collective-permute-start | bytes 196616 | tf_op jit(solution)/shard_map/ppermute | solution.py:298

commit v4 on v3

--- a/solution.py
+++ b/solution.py
@@ -15,9 +15,10 @@
 AXES = EX + EY
 PLANE = ("y_lo", "y_hi", "z")
 OWNERS = ("x", "core", "z")
-COLUMNS = 512
+COLUMNS = 1024
 ROWS = 32
 LANES = 128
+SHIFT = 1.5 * 2.0**23
 
 
 def sine_coefficients(terms):
@@ -53,6 +54,7 @@
     phi,
     argument,
     squares,
+    mixed,
     sums,
     sems,
 ):
@@ -60,37 +62,41 @@
     rows = phi.shape[0]
     chunks = feats // COLUMNS
     large = [
+        pltpu.make_async_copy(factor_hbm.at[e], factor.at[e], sems.at[e]) for e in range(experts)
+    ]
+    comps = noise.shape[1]
+    small = [
         pltpu.make_async_copy(
-            factor_hbm.at[e, :, pl.ds(n * COLUMNS, COLUMNS)],
-            factor.at[e, :, pl.ds(n * COLUMNS, COLUMNS)],
-            sems.at[e * chunks + n],
+            mean_hbm.at[e], means.at[:, pl.ds(e * comps, comps)], sems.at[experts + e]
         )
         for e in range(experts)
-        for n in range(chunks)
     ]
-    mean_copy = pltpu.make_async_copy(mean_hbm, means, sems.at[experts * chunks])
-    for copy in large + [mean_copy]:
+    for copy in small + large:
         copy.start()
 
     turn = 1.0 / (2.0 * math.pi)
     a0, a1, a2 = split(settings[...])
     b0, b1, b2 = split(frequencies[...] * turn)
+    row = lax.broadcasted_iota(jnp.int32, frequencies.shape, 0)
+    p0, p1, p2 = (p.astype(jnp.float32) for p in split(phases[...] * turn))
+    offset = jnp.where(row == 0, p0, jnp.where(row == 1, p1, jnp.where(row == 2, p2, 0.0)))
+    ones = (lax.broadcasted_iota(jnp.int32, settings.shape, 0) < 3).astype(jnp.bfloat16)
     argument[...] = lax.dot_general(
-        jnp.concatenate([a0, a0, a1, a1, a0, a2], 0),
-        jnp.concatenate([b0, b1, b0, b1, b2, b0], 0),
+        jnp.concatenate([a0, a0, a1, a1, a0, a2, ones], 0),
+        jnp.concatenate([b0, b1, b0, b1, b2, b0, offset.astype(jnp.bfloat16)], 0),
         (((0,), (0,)), ((), ())),
         preferred_element_type=jnp.float32,
     )
     amplitude = math.sqrt(2.0 / feats)
-    coefficients = [c * amplitude for c in sine_coefficients(5)]
+    coefficients = [c * amplitude for c in sine_coefficients(4)]
 
     def feature_rows(r, carry):
         block = pl.ds(pl.multiple_of(r * ROWS, ROWS), ROWS)
         total = jnp.zeros((ROWS, LANES), jnp.float32)
         for c in range(feats // 512):
             span = slice(c * 512, (c + 1) * 512)
-            turns = argument[block, span] + phases[:, span] * turn
-            turns = turns - jnp.round(turns)
+            turns = argument[block, span]
+            turns = turns - ((turns + SHIFT) - SHIFT)
             w = 0.25 - jnp.abs(turns)
             square = w * w
             poly = coefficients[-1]
@@ -107,9 +113,12 @@
 
     lax.fori_loop(0, rows // ROWS, feature_rows, 0)
 
+    for copy in small:
+        copy.wait()
+    mixed[...] = jnp.dot(phi[...], means[...], preferred_element_type=jnp.float32)
     for e in range(experts):
+        large[e].wait()
         for n in range(chunks):
-            large[e * chunks + n].wait()
             projected = jnp.dot(
                 phi[...],
                 factor[e, :, n * COLUMNS : (n + 1) * COLUMNS],
@@ -120,21 +129,19 @@
             for j in range(1, COLUMNS // LANES):
                 total = total + projected[:, j * LANES : (j + 1) * LANES]
             squares[e] = total if n == 0 else squares[e] + total
-    mean_copy.wait()
 
     step = 128
     for m in range(rows // step):
         block = slice(m * step, (m + 1) * step)
         prior = noise[...] + scale[...] * jnp.sum(squares[experts, block, :], axis=1, keepdims=True)
-        log_prior = jnp.log(prior)
         inv_prior = 1.0 / prior
         numer = jnp.zeros((step, LANES), jnp.float32)
         denom = inv_prior * (1.0 / devices)
         for e in range(experts):
             variance = noise[...] + scale[...] * jnp.sum(squares[e, block, :], axis=1, keepdims=True)
-            mean = jnp.dot(phi[block, :], means[e], preferred_element_type=jnp.float32)
-            robust = jnp.maximum(0.5 * (log_prior - jnp.log(variance)), 0.0)
+            mean = mixed[block, e * comps : (e + 1) * comps]
             inv_variance = 1.0 / variance
+            robust = jnp.maximum(0.5 * jnp.log(prior * inv_variance), 0.0)
             numer = numer + robust * inv_variance * mean
             denom = denom + robust * (inv_variance - inv_prior)
         sums[m] = jnp.stack([numer.reshape(-1, 16, LANES), denom.reshape(-1, 16, LANES)], axis=1)
@@ -158,12 +165,13 @@
         out_specs=(pl.BlockSpec(memory_space=pltpu.VMEM),) * 2,
         scratch_shapes=[
             pltpu.VMEM((experts, feats, feats), bf16),
-            pltpu.VMEM((experts, feats, comps), bf16),
+            pltpu.VMEM((feats, experts * comps), bf16),
             pltpu.VMEM((rows, feats), bf16),
             pltpu.VMEM((rows, feats), f32),
             pltpu.VMEM((experts + 1, rows, comps), f32),
+            pltpu.VMEM((rows, experts * comps), f32),
             pltpu.VMEM((4, 8, 2, 16, comps), f32),
-            pltpu.SemaphoreType.DMA((experts * (feats // COLUMNS) + 1,)),
+            pltpu.SemaphoreType.DMA((2 * experts,)),
         ],
         compiler_params=pltpu.CompilerParams(vmem_limit_bytes=48 * 2**20),
         cost_estimate=pl.CostEstimate(

time: 69 us -> 69 us (level)
  Pallas kernels: 21 us -> 20 us
  waiting for transfers between devices: 6.2 us -> 7.13 us
    pallas_call x1, Pallas kernels: 14.8 us -> 13.9 us  [experts_sums(): pl.pallas_call(functools.partial(experts_kernel, devices), out_shape=(hal...]
    all_to_all x1, waiting for transfers between devices: 0.48 us -> 1.42 us  [per_device(): lax.all_to_all(relay(component_basis, 8), EY, split_axis=0, concat_axis=0...]
    all_to_all x1, blocking collectives: 14 us -> 15 us  [per_device(): lax.all_to_all(copies, OWNERS, split_axis=0, concat_axis=0, tiled=True)]
    all_to_all x1, blocking collectives: 13.4 us -> 12.5 us  [per_device(): parts = lax.all_to_all(mine, PLANE, split_axis=0, concat_axis=0, tiled=True)]
  transfers between devices with their start and end apart: 5 -> 5, of which waited for: 4 -> 4; matrix products, arithmetic and copies ran while one was open for 0% -> 0% of each run, Pallas kernels for 22% -> 20%
where the time goes in v4:
time: 69 us; the launch traced here: 68.7 us
  blocking collectives  27.5 us (40%)
  Pallas kernels  20 us (29%)
  starting transfers between devices  13.6 us (20%)
  waiting for transfers between devices  7.13 us (10%)
    all_to_all x1, blocking collectives, per_device(): lax.all_to_all(copies, OWNERS, split_axis=0, concat_axis=0, tiled=True)  15 us
    pallas_call x1, Pallas kernels, experts_sums(): pl.pallas_call(functools.partial(experts_kernel, devices), out_shape=(hal...  13.9 us
    all_to_all x1, blocking collectives, per_device(): parts = lax.all_to_all(mine, PLANE, split_axis=0, concat_axis=0, tiled=True)  12.5 us
    all_to_all x1, starting transfers between devices, per_device(): lax.all_to_all(relay(component_basis, 8), EY, split_axis=0, concat_axis=0...  8.64 us
    ppermute x3, waiting for transfers between devices, per_device(): mine = mine + lax.ppermute(part, 'x', [(i, i ^ mask) for i in range(4)])  4.56 us
    ppermute x3, starting transfers between devices, per_device(): mine = mine + lax.ppermute(part, 'x', [(i, i ^ mask) for i in range(4)])  3.94 us
    pallas_call x1, Pallas kernels, stock_of(): pl.pallas_call(stock_kernel, out_shape=jax.ShapeDtypeStruct((rows, cells)...  3.7 us
    pallas_call x1, Pallas kernels, relay(): pl.pallas_call(relay_kernel, out_shape=jax.ShapeDtypeStruct(shape, basis....  2.39 us
  transfers between devices with their start and end apart: 5, of which 4 were waited for; matrix products, arithmetic and copies ran while one was open for 0% of the time, Pallas kernels for 20%

profile of v4, /device:TPU:1, one launch (start us, length us, event | category | flops | bytes accessed | tf_op | source)
XLA Modules:
  0.0 68.7 jit_solution(9054637243336058426)
XLA Ops:
  0.0 2.4 %shard_map.91 = bf16[8,16,8192]{2,1,0:T(8,128)(2,1)} custom-call(bf16[16,65536]{1,0:T(8,128)(2,1)} %basis.1), custom_call_target="tpu_custom_call" | custom-call | tf_op jit(solution)/shard_map/pallas_call | solution.py:235
  2.4 0.0 copy-start.1
  2.4 0.0 copy-start.2
  2.4 0.0 copy-start.3
  2.4 0.0 copy-start.4
  2.4 0.0 copy-start.5
  2.5 0.0 copy-start.6
  2.5 8.6 %all-to-all-start = ((bf16[8,16,8192]{2,1,0:T(8,128)(2,1)}), bf16[8,16,8192]{2,1,0:T(8,128)(2,1)S(1)}, u32[]{:S(2)}, u32[]{:S(2)}) async-start(bf16[8,16,8192]{2,1,0:T(8,128)(2,1)} %shard_map.91), calls=%async_computation | async-start | bytes 4194304 | tf_op jit(solution)/shard_map/all_to_all | solution.py:298
  11.1 0.0 copy-done.1
  11.1 0.0 copy-done.2
  11.1 0.0 copy-done.3
  11.1 0.0 copy-done.4
  11.1 0.0 copy-done.5
  11.2 0.0 copy-done.6
  11.2 13.9 %shard_map.92 = (f32[4,4,2,16,128]{4,3,2,1,0:T(8,128)S(1)}, f32[4,4,2,16,128]{4,3,2,1,0:T(8,128)S(1)}) custom-call(f32[16,512]{1,0:T(8,128)S(1)} %bitcast.13, f32[16,2048]{1,0:T(8,128)S(1)} %copy-done.2, f32[1,2048]{1,0:T(1,128)S(1)} %bitcast.14, f32[1,128]{1,0:T(1,128)S(1)} %bitcast.15, f32[1,128]{1,0:T(1,128)S(1)} %bitcast.16, ...), custom_call_target="tpu_custom_call" | custom-call | flops 9126805504 | bytes 17825792 | tf_op jit(solution)/shard_map/pallas_call | solution.py:161
  25.1 0.0 copy-start
  25.1 1.0 %collective-permute-start = (f32[4,4,2,16,128]{4,3,2,1,0:T(8,128)S(1)}, f32[4,4,2,16,128]{4,3,2,1,0:T(8,128)S(1)}, u32[]{:S(2)}, u32[]{:S(2)}) collective-permute-start(f32[4,4,2,16,128]{4,3,2,1,0:T(8,128)S(1)} %get-tuple-element.14), channel_id=1, source_target_pairs={{0,8},{8,0},{1,9},{9,1},{2,10},{10,2},{3,11},{11,3},{4,12},{12,4},... | collective-permute-start | bytes 786440 | tf_op jit(solution)/shard_map/ppermute | solution.py:303
  26.1 1.2 %collective-permute-done.got_ref = f32[4,4,2,16,128]{4,3,2,1,0:T(8,128)S(1)} collective-permute-done((f32[4,4,2,16,128]{4,3,2,1,0:T(8,128)S(1)}, f32[4,4,2,16,128]{4,3,2,1,0:T(8,128)S(1)}, u32[]{:S(2)}, u32[]{:S(2)}) %collective-permute-start) | collective-permute-done | bytes 262176 | tf_op jit(solution)/shard_map/ppermute | solution.py:303
  27.3 1.3 %collective-permute-start.1 = (f32[4,2,16,128]{3,2,1,0:T(8,128)S(1)}, f32[4,2,16,128]{3,2,1,0:T(8,128)S(1)}, u32[]{:S(2)}, u32[]{:S(2)}) collective-permute-start(f32[4,2,16,128]{3,2,1,0:T(8,128)S(1)} %get-tuple-element.16), channel_id=1, source_target_pairs={{0,16},{16,0},{32,48},{48,32},{1,17},{17,1},{33,49},{49,33},{2,18}... | collective-permute-start | bytes 196616 | tf_op jit(solution)/shard_map/ppermute | solution.py:306
  28.6 2.5 %collective-permute-start.2 = (f32[4,2,16,128]{3,2,1,0:T(8,128)S(1)}, f32[4,2,16,128]{3,2,1,0:T(8,128)S(1)}, u32[]{:S(2)}, u32[]{:S(2)}) collective-permute-start(f32[4,2,16,128]{3,2,1,0:T(8,128)S(1)} %get-tuple-element.17), channel_id=1, source_target_pairs={{0,32},{16,48},{32,0},{48,16},{1,33},{17,49},{33,1},{49,17},{2,34}... | collective-permute-start | bytes 196616 | tf_op jit(solution)/shard_map/ppermute | solution.py:306
  31.1 0.2 collective-permute-start.3
  31.3 0.0 collective-permute-done.1
  31.3 3.0 %collective-permute-done.2 = f32[4,2,16,128]{3,2,1,0:T(8,128)S(1)} collective-permute-done((f32[4,2,16,128]{3,2,1,0:T(8,128)S(1)}, f32[4,2,16,128]{3,2,1,0:T(8,128)S(1)}, u32[]{:S(2)}, u32[]{:S(2)}) %collective-permute-start.2) | collective-permute-done | bytes 65568 | tf_op jit(solution)/shard_map/ppermute | solution.py:306
  34.3 1.5 %collective-permute-done.3 = f32[4,2,16,128]{3,2,1,0:T(8,128)S(1)} collective-permute-done((f32[4,2,16,128]{3,2,1,0:T(8,128)S(1)}, f32[4,2,16,128]{3,2,1,0:T(8,128)S(1)}, u32[]{:S(2)}, u32[]{:S(2)}) %collective-permute-start.3) | collective-permute-done | bytes 65568 | tf_op jit(solution)/shard_map/ppermute | solution.py:306
  35.8 1.4 %all-to-all-done = bf16[8,16,8192]{2,1,0:T(8,128)(2,1)S(1)} async-done(((bf16[8,16,8192]{2,1,0:T(8,128)(2,1)}), bf16[8,16,8192]{2,1,0:T(8,128)(2,1)S(1)}, u32[]{:S(2)}, u32[]{:S(2)}) %all-to-all-start) | async-done | bytes 2097184 | tf_op jit(solution)/shard_map/all_to_all | solution.py:298
  37.3 12.5 %all_to_all.15 = f32[16,2,16,128]{3,2,1,0:T(8,128)S(1)} all-to-all(f32[16,2,16,128]{3,2,1,0:T(8,128)S(1)} %bitcast.17), channel_id=1, replica_groups=mesh['y_lo'=2,'x'=4,'core'=2,'y_hi'=2,'z'=4] {'y_lo','y_hi','z'}, dimensions={0} | all-to-all | bytes 524288 | tf_op jit(solution)/shard_map/all_to_all | solution.py:309
  49.8 15.0 %all_to_all.16 = bf16[32,16,128]{2,1,0:T(8,128)(2,1)S(1)} all-to-all(bf16[32,16,128]{2,1,0:T(8,128)(2,1)S(1)} %broadcast_in_dim.31), channel_id=1, replica_groups=mesh['y_lo'=2,'x'=4,'core'=2,'y_hi'=2,'z'=4] {'x','core','z'}, dimensions={0} | all-to-all | bytes 262144 | tf_op jit(solution)/shard_map/all_to_all | solution.py:313
  64.8 0.0 copy-done
  64.8 3.7 %shard_map.94 = bf16[512,8192]{1,0:T(8,128)(2,1)} custom-call(bf16[512,128]{1,0:T(8,128)(2,1)S(1)} %bitcast.11, bf16[128,8192]{1,0:T(8,128)(2,1)S(1)} %bitcast.10, f32[1,8192]{1,0:T(1,128)S(1)} %bitcast.12), custom_call_target="tpu_custom_call" | custom-call | flops 1073741824 | bytes 8388608 | tf_op jit(solution)/shard_map/pallas_call | solution.py:270
  (6 shorter events, 0.1 us)
Async XLA Ops:
  2.4 8.7 %copy-start.1 = (bf16[2,2048,128]{2,1,0:T(8,128)(2,1)S(1)}, bf16[2,2048,128]{2,1,0:T(8,128)(2,1)}, u32[]{:S(2)}) copy-start(bf16[2,2048,128]{2,1,0:T(8,128)(2,1)} %mean_hbm.1) | copy-start | bytes 3145732
  2.4 8.7 %copy-start.2 = (f32[16,2048]{1,0:T(8,128)S(1)}, f32[16,2048]{1,0:T(8,128)}, u32[]{:S(2)}) copy-start(f32[16,2048]{1,0:T(8,128)} %frequencies.1) | copy-start | bytes 393220
  2.4 8.7 %copy-start.3 = (f32[512,16]{0,1:T(8,128)S(1)}, f32[512,16]{0,1:T(8,128)}, u32[]{:S(2)}) copy-start(f32[512,16]{0,1:T(8,128)} %param.9) | copy-start | bytes 98308
  2.4 8.7 %copy-start.4 = (f32[2048]{0:T(1024)S(1)}, f32[2048]{0:T(1024)}, u32[]{:S(2)}) copy-start(f32[2048]{0:T(1024)} %param.11) | copy-start | bytes 24580
  2.4 8.7 %copy-start.5 = (f32[128]{0:T(128)S(1)}, f32[128]{0:T(128)}, u32[]{:S(2)}) copy-start(f32[128]{0:T(128)} %param.12) | copy-start | bytes 1540
  2.5 8.7 %copy-start.6 = (f32[128]{0:T(128)S(1)}, f32[128]{0:T(128)}, u32[]{:S(2)}) copy-start(f32[128]{0:T(128)} %param.13) | copy-start | bytes 1540
  2.5 34.8 %all-to-all-start = ((bf16[8,16,8192]{2,1,0:T(8,128)(2,1)}), bf16[8,16,8192]{2,1,0:T(8,128)(2,1)S(1)}, u32[]{:S(2)}, u32[]{:S(2)}) async-start(bf16[8,16,8192]{2,1,0:T(8,128)(2,1)} %shard_map.91), calls=%async_computation | async-start | bytes 4194304 | tf_op jit(solution)/shard_map/all_to_all | solution.py:298
  25.1 39.8 %copy-start = (f32[8192]{0:T(1024)S(1)}, f32[8192]{0:T(1024)}, u32[]{:S(2)}) copy-start(f32[8192]{0:T(1024)} %param.17) | copy-start | bytes 98308
  25.1 2.2 %collective-permute-start = (f32[4,4,2,16,128]{4,3,2,1,0:T(8,128)S(1)}, f32[4,4,2,16,128]{4,3,2,1,0:T(8,128)S(1)}, u32[]{:S(2)}, u32[]{:S(2)}) collective-permute-start(f32[4,4,2,16,128]{4,3,2,1,0:T(8,128)S(1)} %get-tuple-element.14), channel_id=1, source_target_pairs={{0,8},{8,0},{1,9},{9,1},{2,10},{10,2},{3,11},{11,3},{4,12},{12,4},... | collective-permute-start | bytes 786440 | tf_op jit(solution)/shard_map/ppermute | solution.py:303
  27.3 3.9 %collective-permute-start.1 = (f32[4,2,16,128]{3,2,1,0:T(8,128)S(1)}, f32[4,2,16,128]{3,2,1,0:T(8,128)S(1)}, u32[]{:S(2)}, u32[]{:S(2)}) collective-permute-start(f32[4,2,16,128]{3,2,1,0:T(8,128)S(1)} %get-tuple-element.16), channel_id=1, source_target_pairs={{0,16},{16,0},{32,48},{48,32},{1,17},{17,1},{33,49},{49,33},{2,18}... | collective-permute-start | bytes 196616 | tf_op jit(solution)/shard_map/ppermute | solution.py:306
  28.6 5.7 %collective-permute-start.2 = (f32[4,2,16,128]{3,2,1,0:T(8,128)S(1)}, f32[4,2,16,128]{3,2,1,0:T(8,128)S(1)}, u32[]{:S(2)}, u32[]{:S(2)}) collective-permute-start(f32[4,2,16,128]{3,2,1,0:T(8,128)S(1)} %get-tuple-element.17), channel_id=1, source_target_pairs={{0,32},{16,48},{32,0},{48,16},{1,33},{17,49},{33,1},{49,17},{2,34}... | collective-permute-start | bytes 196616 | tf_op jit(solution)/shard_map/ppermute | solution.py:306
  31.1 4.8 %collective-permute-start.3 = (f32[4,2,16,128]{3,2,1,0:T(8,128)S(1)}, f32[4,2,16,128]{3,2,1,0:T(8,128)S(1)}, u32[]{:S(2)}, u32[]{:S(2)}) collective-permute-start(f32[4,2,16,128]{3,2,1,0:T(8,128)S(1)} %get-tuple-element.18), channel_id=1, source_target_pairs={{0,48},{16,32},{32,16},{48,0},{1,49},{17,33},{33,17},{49,1},{2,50}... | collective-permute-start | bytes 196616 | tf_op jit(solution)/shard_map/ppermute | solution.py:306

commit v5 on v4

--- a/solution.py
+++ b/solution.py
@@ -11,10 +11,10 @@
 from jax.sharding import PartitionSpec as P
 
 EX = ("y_lo", "x", "core")
-EY = ("y_hi", "z")
+EY = ("y_hi", "z_hi", "z_lo")
 AXES = EX + EY
-PLANE = ("y_lo", "y_hi", "z")
-OWNERS = ("x", "core", "z")
+PLANE = ("y_lo", "y_hi", "z_hi", "z_lo")
+OWNERS = ("x", "core", "z_lo")
 COLUMNS = 1024
 ROWS = 32
 LANES = 128
@@ -88,7 +88,7 @@
         preferred_element_type=jnp.float32,
     )
     amplitude = math.sqrt(2.0 / feats)
-    coefficients = [c * amplitude for c in sine_coefficients(4)]
+    coefficients = [c * amplitude for c in sine_coefficients(5)]
 
     def feature_rows(r, carry):
         block = pl.ds(pl.multiple_of(r * ROWS, ROWS), ROWS)
@@ -144,12 +144,12 @@
             robust = jnp.maximum(0.5 * jnp.log(prior * inv_variance), 0.0)
             numer = numer + robust * inv_variance * mean
             denom = denom + robust * (inv_variance - inv_prior)
-        sums[m] = jnp.stack([numer.reshape(-1, 16, LANES), denom.reshape(-1, 16, LANES)], axis=1)
+        sums[m] = jnp.stack([numer.reshape(-1, 32, LANES), denom.reshape(-1, 32, LANES)], axis=1)
 
     core = lax.axis_index("core")
     for x in range(4):
-        keep_ref[x] = sums[x, pl.ds(4 * core, 4)]
-        send_ref[x] = sums[x, pl.ds(4 * (1 - core), 4)]
+        keep_ref[x] = sums[x, pl.ds(2 * core, 2)]
+        send_ref[x] = sums[x, pl.ds(2 * (1 - core), 2)]
 
 
 def experts_sums(devices, settings, frequencies, phases, noise_var, signal_scale, cov_factor, post_mean):
@@ -157,7 +157,7 @@
     rows = settings.shape[0]
     comps = noise_var.shape[0]
     f32, bf16 = jnp.float32, jnp.bfloat16
-    half = jax.ShapeDtypeStruct((4, 4, 2, 16, comps), f32)
+    half = jax.ShapeDtypeStruct((4, 2, 2, 32, comps), f32)
     return pl.pallas_call(
         functools.partial(experts_kernel, devices),
         out_shape=(half, half),
@@ -170,7 +170,7 @@
             pltpu.VMEM((rows, feats), f32),
             pltpu.VMEM((experts + 1, rows, comps), f32),
             pltpu.VMEM((rows, experts * comps), f32),
-            pltpu.VMEM((4, 8, 2, 16, comps), f32),
+            pltpu.VMEM((4, 4, 2, 32, comps), f32),
             pltpu.SemaphoreType.DMA((2 * experts,)),
         ],
         compiler_params=pltpu.CompilerParams(vmem_limit_bytes=48 * 2**20),
@@ -211,6 +211,34 @@
     )(keep, got)
 
 
+def pack_kernel(*refs):
+    parts, out_ref = refs[:-1], refs[-1]
+    groups = parts[0].shape[0]
+    for g in range(groups):
+        numer, denom = (
+            (parts[0][g, k] + parts[1][g, k]) + (parts[2][g, k] + parts[3][g, k]) for k in range(2)
+        )
+        high = numer.astype(jnp.bfloat16)
+        low = (numer - high.astype(jnp.float32)).astype(jnp.bfloat16)
+        denom = denom.astype(jnp.bfloat16)
+        for copy in range(out_ref.shape[0] // groups):
+            out_ref[copy * groups + g, 0] = high
+            out_ref[copy * groups + g, 1] = low
+            out_ref[copy * groups + g, 2] = denom
+
+
+def pack(parts, devices):
+    _, _, depth, comps = parts[0].shape
+    vmem = pl.BlockSpec(memory_space=pltpu.VMEM)
+    return pl.pallas_call(
+        pack_kernel,
+        out_shape=jax.ShapeDtypeStruct((devices, 3, depth, comps), jnp.bfloat16),
+        in_specs=[vmem] * len(parts),
+        out_specs=vmem,
+        compiler_params=pltpu.CompilerParams(vmem_limit_bytes=8 * 2**20),
+    )(*parts)
+
+
 def relay_kernel(basis, out_ref, held, read_sems, write_sems):
     devices, _, cells = out_ref.shape
     reads = [
@@ -302,14 +330,17 @@
     )
     got = lax.ppermute(send, "core", [(0, 1), (1, 0)])
     mine, *sends = combine(keep, got)
-    for mask, part in enumerate(sends, 1):
-        mine = mine + lax.ppermute(part, "x", [(i, i ^ mask) for i in range(4)])
-    relaid, mine = lax.optimization_barrier((relaid, mine))
-    mine = jnp.broadcast_to(mine[None], (4,) + mine.shape).reshape((16,) + mine.shape[1:])
-    parts = lax.all_to_all(mine, PLANE, split_axis=0, concat_axis=0, tiled=True)
-    numer, denom = jnp.sum(parts, axis=0)
+    parts = [mine] + [
+        lax.ppermute(part, "x", [(i, i ^ mask) for i in range(4)])
+        for mask, part in enumerate(sends, 1)
+    ]
+    packed = pack(parts, 16)
+    relaid, packed = lax.optimization_barrier((relaid, packed))
+    got = lax.all_to_all(packed, PLANE, split_axis=0, concat_axis=0, tiled=True)
+    high, low, denom = jnp.sum(got.astype(jnp.float32), axis=0)
+    numer = high + low
     mine = (numer / denom).astype(jnp.bfloat16)
-    copies = jnp.broadcast_to(mine[None], (32,) + mine.shape)
+    copies = jnp.broadcast_to(mine[None], (16,) + mine.shape)
     weights = lax.all_to_all(copies, OWNERS, split_axis=0, concat_axis=0, tiled=True)
     return stock_of(weights.reshape(settings.shape[0], -1), relaid, mean_field)
 
@@ -327,7 +358,7 @@
         P(AXES),
     )
     out_specs = P(None, AXES)
-    fine = Mesh(np.asarray(mesh.devices).reshape(2, 4, 2, 2, 4), AXES)
+    fine = Mesh(np.asarray(mesh.devices).reshape(2, 4, 2, 2, 2, 2), AXES)
     return jax.shard_map(
         functools.partial(per_device, mesh.size),
         mesh=fine,

time: 69 us -> 68 us (0.986)
  blocking collectives: 27.5 us -> 26.5 us
    all_to_all x1, blocking collectives: 15 us -> 12.9 us  [per_device(): lax.all_to_all(copies, OWNERS, split_axis=0, concat_axis=0, tiled=True)]
    all_to_all x1, blocking collectives: 12.5 us -> 13.6 us  [per_device(): got = lax.all_to_all(packed, PLANE, split_axis=0, concat_axis=0, tiled=True)]
  transfers between devices with their start and end apart: 5 -> 5, of which waited for: 4 -> 4; matrix products, arithmetic and copies ran while one was open for 0% -> 0% of each run, Pallas kernels for 20% -> 21%
where the time goes in v5:
time: 68 us; the launch traced here: 67.8 us
  blocking collectives  26.5 us (39%)
  Pallas kernels  20.4 us (30%)
  starting transfers between devices  13.6 us (20%)
  waiting for transfers between devices  6.83 us (10%)
    pallas_call x1, Pallas kernels, experts_sums(): pl.pallas_call(functools.partial(experts_kernel, devices), out_shape=(hal...  14.2 us
    all_to_all x1, blocking collectives, per_device(): got = lax.all_to_all(packed, PLANE, split_axis=0, concat_axis=0, tiled=True)  13.6 us
    all_to_all x1, blocking collectives, per_device(): lax.all_to_all(copies, OWNERS, split_axis=0, concat_axis=0, tiled=True)  12.9 us
    all_to_all x1, starting transfers between devices, per_device(): lax.all_to_all(relay(component_basis, 8), EY, split_axis=0, concat_axis=0...  8.64 us
    ppermute x3, waiting for transfers between devices, per_device(): lax.ppermute(part, 'x', [(i, i ^ mask) for i in range(4)])  4.56 us
    ppermute x3, starting transfers between devices, per_device(): lax.ppermute(part, 'x', [(i, i ^ mask) for i in range(4)])  3.94 us
    pallas_call x1, Pallas kernels, stock_of(): pl.pallas_call(stock_kernel, out_shape=jax.ShapeDtypeStruct((rows, cells)...  3.7 us
    pallas_call x1, Pallas kernels, relay(): pl.pallas_call(relay_kernel, out_shape=jax.ShapeDtypeStruct(shape, basis....  2.39 us
  transfers between devices with their start and end apart: 5, of which 4 were waited for; matrix products, arithmetic and copies ran while one was open for 0% of the time, Pallas kernels for 21%

profile of v5, /device:TPU:1, one launch (start us, length us, event | category | flops | bytes accessed | tf_op | source)
XLA Modules:
  0.0 67.8 jit_solution(635694695143405583)
XLA Ops:
  0.0 2.4 %shard_map.91 = bf16[8,16,8192]{2,1,0:T(8,128)(2,1)} custom-call(bf16[16,65536]{1,0:T(8,128)(2,1)} %basis.1), custom_call_target="tpu_custom_call" | custom-call | tf_op jit(solution)/shard_map/pallas_call | solution.py:263
  2.4 0.0 copy-start.1
  2.4 0.0 copy-start.2
  2.4 0.0 copy-start.3
  2.4 0.0 copy-start.4
  2.4 0.0 copy-start.5
  2.5 0.0 copy-start.6
  2.5 8.6 %all-to-all-start = ((bf16[8,16,8192]{2,1,0:T(8,128)(2,1)}), bf16[8,16,8192]{2,1,0:T(8,128)(2,1)S(1)}, u32[]{:S(2)}, u32[]{:S(2)}) async-start(bf16[8,16,8192]{2,1,0:T(8,128)(2,1)} %shard_map.91), calls=%async_computation | async-start | bytes 4194304 | tf_op jit(solution)/shard_map/all_to_all | solution.py:326
  11.1 0.0 copy-done.1
  11.1 0.0 copy-done.2
  11.1 0.0 copy-done.3
  11.1 0.0 copy-done.4
  11.1 0.0 copy-done.5
  11.2 0.0 copy-done.6
  11.2 14.2 %shard_map.92 = (f32[4,2,2,32,128]{4,3,2,1,0:T(8,128)S(1)}, f32[4,2,2,32,128]{4,3,2,1,0:T(8,128)S(1)}) custom-call(f32[16,512]{1,0:T(8,128)S(1)} %bitcast.12, f32[16,2048]{1,0:T(8,128)S(1)} %copy-done.2, f32[1,2048]{1,0:T(1,128)S(1)} %bitcast.13, f32[1,128]{1,0:T(1,128)S(1)} %bitcast.14, f32[1,128]{1,0:T(1,128)S(1)} %bitcast.15, ...), custom_call_target="tpu_custom_call" | custom-call | flops 9126805504 | bytes 17825792 | tf_op jit(solution)/shard_map/pallas_call | solution.py:161
  25.4 0.0 copy-start
  25.4 1.0 %collective-permute-start = (f32[4,2,2,32,128]{4,3,2,1,0:T(8,128)S(1)}, f32[4,2,2,32,128]{4,3,2,1,0:T(8,128)S(1)}, u32[]{:S(2)}, u32[]{:S(2)}) collective-permute-start(f32[4,2,2,32,128]{4,3,2,1,0:T(8,128)S(1)} %get-tuple-element.14), channel_id=1, source_target_pairs={{0,8},{8,0},{1,9},{9,1},{2,10},{10,2},{3,11},{11,3},{4,12},{12,4},... | collective-permute-start | bytes 786440 | tf_op jit(solution)/shard_map/ppermute | solution.py:331
  26.4 1.2 %collective-permute-done.got_ref = f32[4,2,2,32,128]{4,3,2,1,0:T(8,128)S(1)} collective-permute-done((f32[4,2,2,32,128]{4,3,2,1,0:T(8,128)S(1)}, f32[4,2,2,32,128]{4,3,2,1,0:T(8,128)S(1)}, u32[]{:S(2)}, u32[]{:S(2)}) %collective-permute-start) | collective-permute-done | bytes 262176 | tf_op jit(solution)/shard_map/ppermute | solution.py:331
  27.6 1.3 %collective-permute-start.1 = (f32[2,2,32,128]{3,2,1,0:T(8,128)S(1)}, f32[2,2,32,128]{3,2,1,0:T(8,128)S(1)}, u32[]{:S(2)}, u32[]{:S(2)}) collective-permute-start(f32[2,2,32,128]{3,2,1,0:T(8,128)S(1)} %get-tuple-element.16), channel_id=1, source_target_pairs={{0,16},{16,0},{32,48},{48,32},{1,17},{17,1},{33,49},{49,33},{2,18}... | collective-permute-start | bytes 196616 | tf_op jit(solution)/shard_map/ppermute | solution.py:334
  28.9 2.5 %collective-permute-start.2 = (f32[2,2,32,128]{3,2,1,0:T(8,128)S(1)}, f32[2,2,32,128]{3,2,1,0:T(8,128)S(1)}, u32[]{:S(2)}, u32[]{:S(2)}) collective-permute-start(f32[2,2,32,128]{3,2,1,0:T(8,128)S(1)} %get-tuple-element.17), channel_id=1, source_target_pairs={{0,32},{16,48},{32,0},{48,16},{1,33},{17,49},{33,1},{49,17},{2,34}... | collective-permute-start | bytes 196616 | tf_op jit(solution)/shard_map/ppermute | solution.py:334
  31.4 0.2 collective-permute-start.3
  31.5 0.0 collective-permute-done.1.refs_1_
  31.6 3.0 %collective-permute-done.2.refs_2_ = f32[2,2,32,128]{3,2,1,0:T(8,128)S(1)} collective-permute-done((f32[2,2,32,128]{3,2,1,0:T(8,128)S(1)}, f32[2,2,32,128]{3,2,1,0:T(8,128)S(1)}, u32[]{:S(2)}, u32[]{:S(2)}) %collective-permute-start.2) | collective-permute-done | bytes 65568 | tf_op jit(solution)/shard_map/ppermute | solution.py:334
  34.6 1.5 %collective-permute-done.3.refs_3_ = f32[2,2,32,128]{3,2,1,0:T(8,128)S(1)} collective-permute-done((f32[2,2,32,128]{3,2,1,0:T(8,128)S(1)}, f32[2,2,32,128]{3,2,1,0:T(8,128)S(1)}, u32[]{:S(2)}, u32[]{:S(2)}) %collective-permute-start.3) | collective-permute-done | bytes 65568 | tf_op jit(solution)/shard_map/ppermute | solution.py:334
  36.1 1.1 %all-to-all-done = bf16[8,16,8192]{2,1,0:T(8,128)(2,1)S(1)} async-done(((bf16[8,16,8192]{2,1,0:T(8,128)(2,1)}), bf16[8,16,8192]{2,1,0:T(8,128)(2,1)S(1)}, u32[]{:S(2)}, u32[]{:S(2)}) %all-to-all-start) | async-done | bytes 2097184 | tf_op jit(solution)/shard_map/all_to_all | solution.py:326
  37.3 13.6 %all_to_all.15 = bf16[16,3,32,128]{3,2,1,0:T(8,128)(2,1)S(1)} all-to-all(bf16[16,3,32,128]{3,2,1,0:T(8,128)(2,1)S(1)} %shard_map.94), channel_id=1, replica_groups=mesh['y_lo'=2,'x'=4,'core'=2,'y_hi'=2,'z_hi'=2,'z_lo'=2] {'y_lo','y_hi',..., dimensions={0} | all-to-all | bytes 786432 | tf_op jit(solution)/shard_map/all_to_all | solution.py:339
  50.9 0.1 convert_reduce_fusion
  51.0 12.9 %all_to_all.16 = bf16[16,32,128]{2,1,0:T(8,128)(2,1)S(1)} all-to-all(bf16[16,32,128]{2,1,0:T(8,128)(2,1)S(1)} %broadcast_in_dim.24), channel_id=1, replica_groups=mesh['y_lo'=2,'x'=4,'core'=2,'y_hi'=2,'z_hi'=2,'z_lo'=2] {'x','core','z_..., dimensions={0} | all-to-all | bytes 262144 | tf_op jit(solution)/shard_map/all_to_all | solution.py:344
  63.9 0.0 copy-done
  63.9 3.7 %shard_map.95 = bf16[512,8192]{1,0:T(8,128)(2,1)} custom-call(bf16[512,128]{1,0:T(8,128)(2,1)S(1)} %bitcast.10, bf16[128,8192]{1,0:T(8,128)(2,1)S(1)} %bitcast.9, f32[1,8192]{1,0:T(1,128)S(1)} %bitcast.11), custom_call_target="tpu_custom_call" | custom-call | flops 1073741824 | bytes 8388608 | tf_op jit(solution)/shard_map/pallas_call | solution.py:298
  (4 shorter events, 0.1 us)
Async XLA Ops:
  2.4 8.7 %copy-start.1 = (bf16[2,2048,128]{2,1,0:T(8,128)(2,1)S(1)}, bf16[2,2048,128]{2,1,0:T(8,128)(2,1)}, u32[]{:S(2)}) copy-start(bf16[2,2048,128]{2,1,0:T(8,128)(2,1)} %mean_hbm.1) | copy-start | bytes 3145732
  2.4 8.7 %copy-start.2 = (f32[16,2048]{1,0:T(8,128)S(1)}, f32[16,2048]{1,0:T(8,128)}, u32[]{:S(2)}) copy-start(f32[16,2048]{1,0:T(8,128)} %frequencies.1) | copy-start | bytes 393220
  2.4 8.7 %copy-start.3 = (f32[512,16]{0,1:T(8,128)S(1)}, f32[512,16]{0,1:T(8,128)}, u32[]{:S(2)}) copy-start(f32[512,16]{0,1:T(8,128)} %param.9) | copy-start | bytes 98308
  2.4 8.7 %copy-start.4 = (f32[2048]{0:T(1024)S(1)}, f32[2048]{0:T(1024)}, u32[]{:S(2)}) copy-start(f32[2048]{0:T(1024)} %param.11) | copy-start | bytes 24580
  2.4 8.7 %copy-start.5 = (f32[128]{0:T(128)S(1)}, f32[128]{0:T(128)}, u32[]{:S(2)}) copy-start(f32[128]{0:T(128)} %param.12) | copy-start | bytes 1540
  2.5 8.7 %copy-start.6 = (f32[128]{0:T(128)S(1)}, f32[128]{0:T(128)}, u32[]{:S(2)}) copy-start(f32[128]{0:T(128)} %param.13) | copy-start | bytes 1540
  2.5 34.8 %all-to-all-start = ((bf16[8,16,8192]{2,1,0:T(8,128)(2,1)}), bf16[8,16,8192]{2,1,0:T(8,128)(2,1)S(1)}, u32[]{:S(2)}, u32[]{:S(2)}) async-start(bf16[8,16,8192]{2,1,0:T(8,128)(2,1)} %shard_map.91), calls=%async_computation | async-start | bytes 4194304 | tf_op jit(solution)/shard_map/all_to_all | solution.py:326
  25.4 38.5 %copy-start = (f32[8192]{0:T(1024)S(1)}, f32[8192]{0:T(1024)}, u32[]{:S(2)}) copy-start(f32[8192]{0:T(1024)} %param.17) | copy-start | bytes 98308
  25.4 2.2 %collective-permute-start = (f32[4,2,2,32,128]{4,3,2,1,0:T(8,128)S(1)}, f32[4,2,2,32,128]{4,3,2,1,0:T(8,128)S(1)}, u32[]{:S(2)}, u32[]{:S(2)}) collective-permute-start(f32[4,2,2,32,128]{4,3,2,1,0:T(8,128)S(1)} %get-tuple-element.14), channel_id=1, source_target_pairs={{0,8},{8,0},{1,9},{9,1},{2,10},{10,2},{3,11},{11,3},{4,12},{12,4},... | collective-permute-start | bytes 786440 | tf_op jit(solution)/shard_map/ppermute | solution.py:331
  27.6 3.9 %collective-permute-start.1 = (f32[2,2,32,128]{3,2,1,0:T(8,128)S(1)}, f32[2,2,32,128]{3,2,1,0:T(8,128)S(1)}, u32[]{:S(2)}, u32[]{:S(2)}) collective-permute-start(f32[2,2,32,128]{3,2,1,0:T(8,128)S(1)} %get-tuple-element.16), channel_id=1, source_target_pairs={{0,16},{16,0},{32,48},{48,32},{1,17},{17,1},{33,49},{49,33},{2,18}... | collective-permute-start | bytes 196616 | tf_op jit(solution)/shard_map/ppermute | solution.py:334
  28.9 5.7 %collective-permute-start.2 = (f32[2,2,32,128]{3,2,1,0:T(8,128)S(1)}, f32[2,2,32,128]{3,2,1,0:T(8,128)S(1)}, u32[]{:S(2)}, u32[]{:S(2)}) collective-permute-start(f32[2,2,32,128]{3,2,1,0:T(8,128)S(1)} %get-tuple-element.17), channel_id=1, source_target_pairs={{0,32},{16,48},{32,0},{48,16},{1,33},{17,49},{33,1},{49,17},{2,34}... | collective-permute-start | bytes 196616 | tf_op jit(solution)/shard_map/ppermute | solution.py:334
  31.4 4.8 %collective-permute-start.3 = (f32[2,2,32,128]{3,2,1,0:T(8,128)S(1)}, f32[2,2,32,128]{3,2,1,0:T(8,128)S(1)}, u32[]{:S(2)}, u32[]{:S(2)}) collective-permute-start(f32[2,2,32,128]{3,2,1,0:T(8,128)S(1)} %get-tuple-element.18), channel_id=1, source_target_pairs={{0,48},{16,32},{32,16},{48,0},{1,49},{17,33},{33,17},{49,1},{2,50}... | collective-permute-start | bytes 196616 | tf_op jit(solution)/shard_map/ppermute | solution.py:334

commit v6 on v5

--- a/solution.py
+++ b/solution.py
@@ -88,7 +88,7 @@
         preferred_element_type=jnp.float32,
     )
     amplitude = math.sqrt(2.0 / feats)
-    coefficients = [c * amplitude for c in sine_coefficients(5)]
+    coefficients = [c * amplitude for c in sine_coefficients(4)]
 
     def feature_rows(r, carry):
         block = pl.ds(pl.multiple_of(r * ROWS, ROWS), ROWS)

time: 68 us -> 68 us (level)
  no operation moved by 1% of the time
where the time goes in v6:
time: 68 us; the launch traced here: 67.8 us
  blocking collectives  26.5 us (39%)
  Pallas kernels  20.1 us (30%)
  starting transfers between devices  13.6 us (20%)
  waiting for transfers between devices  7.12 us (10%)
    pallas_call x1, Pallas kernels, experts_sums(): pl.pallas_call(functools.partial(experts_kernel, devices), out_shape=(hal...  13.9 us
    all_to_all x1, blocking collectives, per_device(): got = lax.all_to_all(packed, PLANE, split_axis=0, concat_axis=0, tiled=True)  13.3 us
    all_to_all x1, blocking collectives, per_device(): lax.all_to_all(copies, OWNERS, split_axis=0, concat_axis=0, tiled=True)  13.2 us
    all_to_all x1, starting transfers between devices, per_device(): lax.all_to_all(relay(component_basis, 8), EY, split_axis=0, concat_axis=0...  8.64 us
    ppermute x3, waiting for transfers between devices, per_device(): lax.ppermute(part, 'x', [(i, i ^ mask) for i in range(4)])  4.56 us
    ppermute x3, starting transfers between devices, per_device(): lax.ppermute(part, 'x', [(i, i ^ mask) for i in range(4)])  3.94 us
    pallas_call x1, Pallas kernels, stock_of(): pl.pallas_call(stock_kernel, out_shape=jax.ShapeDtypeStruct((rows, cells)...  3.7 us
    pallas_call x1, Pallas kernels, relay(): pl.pallas_call(relay_kernel, out_shape=jax.ShapeDtypeStruct(shape, basis....  2.39 us
  transfers between devices with their start and end apart: 5, of which 4 were waited for; matrix products, arithmetic and copies ran while one was open for 0% of the time, Pallas kernels for 21%

profile of v6, /device:TPU:1, one launch (start us, length us, event | category | flops | bytes accessed | tf_op | source)
XLA Modules:
  0.0 67.8 jit_solution(3458670107042120659)
XLA Ops:
  0.0 2.4 %shard_map.91 = bf16[8,16,8192]{2,1,0:T(8,128)(2,1)} custom-call(bf16[16,65536]{1,0:T(8,128)(2,1)} %basis.1), custom_call_target="tpu_custom_call" | custom-call | tf_op jit(solution)/shard_map/pallas_call | solution.py:263
  2.4 0.0 copy-start.1
  2.4 0.0 copy-start.2
  2.4 0.0 copy-start.3
  2.4 0.0 copy-start.4
  2.4 0.0 copy-start.5
  2.5 0.0 copy-start.6
  2.5 8.6 %all-to-all-start = ((bf16[8,16,8192]{2,1,0:T(8,128)(2,1)}), bf16[8,16,8192]{2,1,0:T(8,128)(2,1)S(1)}, u32[]{:S(2)}, u32[]{:S(2)}) async-start(bf16[8,16,8192]{2,1,0:T(8,128)(2,1)} %shard_map.91), calls=%async_computation | async-start | bytes 4194304 | tf_op jit(solution)/shard_map/all_to_all | solution.py:326
  11.1 0.0 copy-done.1
  11.1 0.0 copy-done.2
  11.1 0.0 copy-done.3
  11.1 0.0 copy-done.4
  11.1 0.0 copy-done.5
  11.2 0.0 copy-done.6
  11.2 13.9 %shard_map.92 = (f32[4,2,2,32,128]{4,3,2,1,0:T(8,128)S(1)}, f32[4,2,2,32,128]{4,3,2,1,0:T(8,128)S(1)}) custom-call(f32[16,512]{1,0:T(8,128)S(1)} %bitcast.12, f32[16,2048]{1,0:T(8,128)S(1)} %copy-done.2, f32[1,2048]{1,0:T(1,128)S(1)} %bitcast.13, f32[1,128]{1,0:T(1,128)S(1)} %bitcast.14, f32[1,128]{1,0:T(1,128)S(1)} %bitcast.15, ...), custom_call_target="tpu_custom_call" | custom-call | flops 9126805504 | bytes 17825792 | tf_op jit(solution)/shard_map/pallas_call | solution.py:161
  25.1 0.0 copy-start
  25.1 1.0 %collective-permute-start = (f32[4,2,2,32,128]{4,3,2,1,0:T(8,128)S(1)}, f32[4,2,2,32,128]{4,3,2,1,0:T(8,128)S(1)}, u32[]{:S(2)}, u32[]{:S(2)}) collective-permute-start(f32[4,2,2,32,128]{4,3,2,1,0:T(8,128)S(1)} %get-tuple-element.14), channel_id=1, source_target_pairs={{0,8},{8,0},{1,9},{9,1},{2,10},{10,2},{3,11},{11,3},{4,12},{12,4},... | collective-permute-start | bytes 786440 | tf_op jit(solution)/shard_map/ppermute | solution.py:331
  26.1 1.2 %collective-permute-done.got_ref = f32[4,2,2,32,128]{4,3,2,1,0:T(8,128)S(1)} collective-permute-done((f32[4,2,2,32,128]{4,3,2,1,0:T(8,128)S(1)}, f32[4,2,2,32,128]{4,3,2,1,0:T(8,128)S(1)}, u32[]{:S(2)}, u32[]{:S(2)}) %collective-permute-start) | collective-permute-done | bytes 262176 | tf_op jit(solution)/shard_map/ppermute | solution.py:331
  27.3 1.3 %collective-permute-start.1 = (f32[2,2,32,128]{3,2,1,0:T(8,128)S(1)}, f32[2,2,32,128]{3,2,1,0:T(8,128)S(1)}, u32[]{:S(2)}, u32[]{:S(2)}) collective-permute-start(f32[2,2,32,128]{3,2,1,0:T(8,128)S(1)} %get-tuple-element.16), channel_id=1, source_target_pairs={{0,16},{16,0},{32,48},{48,32},{1,17},{17,1},{33,49},{49,33},{2,18}... | collective-permute-start | bytes 196616 | tf_op jit(solution)/shard_map/ppermute | solution.py:334
  28.6 2.5 %collective-permute-start.2 = (f32[2,2,32,128]{3,2,1,0:T(8,128)S(1)}, f32[2,2,32,128]{3,2,1,0:T(8,128)S(1)}, u32[]{:S(2)}, u32[]{:S(2)}) collective-permute-start(f32[2,2,32,128]{3,2,1,0:T(8,128)S(1)} %get-tuple-element.17), channel_id=1, source_target_pairs={{0,32},{16,48},{32,0},{48,16},{1,33},{17,49},{33,1},{49,17},{2,34}... | collective-permute-start | bytes 196616 | tf_op jit(solution)/shard_map/ppermute | solution.py:334
  31.1 0.2 collective-permute-start.3
  31.3 0.0 collective-permute-done.1.refs_1_
  31.3 3.0 %collective-permute-done.2.refs_2_ = f32[2,2,32,128]{3,2,1,0:T(8,128)S(1)} collective-permute-done((f32[2,2,32,128]{3,2,1,0:T(8,128)S(1)}, f32[2,2,32,128]{3,2,1,0:T(8,128)S(1)}, u32[]{:S(2)}, u32[]{:S(2)}) %collective-permute-start.2) | collective-permute-done | bytes 65568 | tf_op jit(solution)/shard_map/ppermute | solution.py:334
  34.3 1.5 %collective-permute-done.3.refs_3_ = f32[2,2,32,128]{3,2,1,0:T(8,128)S(1)} collective-permute-done((f32[2,2,32,128]{3,2,1,0:T(8,128)S(1)}, f32[2,2,32,128]{3,2,1,0:T(8,128)S(1)}, u32[]{:S(2)}, u32[]{:S(2)}) %collective-permute-start.3) | collective-permute-done | bytes 65568 | tf_op jit(solution)/shard_map/ppermute | solution.py:334
  35.9 1.4 %all-to-all-done = bf16[8,16,8192]{2,1,0:T(8,128)(2,1)S(1)} async-done(((bf16[8,16,8192]{2,1,0:T(8,128)(2,1)}), bf16[8,16,8192]{2,1,0:T(8,128)(2,1)S(1)}, u32[]{:S(2)}, u32[]{:S(2)}) %all-to-all-start) | async-done | bytes 2097184 | tf_op jit(solution)/shard_map/all_to_all | solution.py:326
  37.3 13.3 %all_to_all.15 = bf16[16,3,32,128]{3,2,1,0:T(8,128)(2,1)S(1)} all-to-all(bf16[16,3,32,128]{3,2,1,0:T(8,128)(2,1)S(1)} %shard_map.94), channel_id=1, replica_groups=mesh['y_lo'=2,'x'=4,'core'=2,'y_hi'=2,'z_hi'=2,'z_lo'=2] {'y_lo','y_hi',..., dimensions={0} | all-to-all | bytes 786432 | tf_op jit(solution)/shard_map/all_to_all | solution.py:339
  50.6 0.1 convert_reduce_fusion
  50.7 13.2 %all_to_all.16 = bf16[16,32,128]{2,1,0:T(8,128)(2,1)S(1)} all-to-all(bf16[16,32,128]{2,1,0:T(8,128)(2,1)S(1)} %broadcast_in_dim.24), channel_id=1, replica_groups=mesh['y_lo'=2,'x'=4,'core'=2,'y_hi'=2,'z_hi'=2,'z_lo'=2] {'x','core','z_..., dimensions={0} | all-to-all | bytes 262144 | tf_op jit(solution)/shard_map/all_to_all | solution.py:344
  63.9 0.0 copy-done
  63.9 3.7 %shard_map.95 = bf16[512,8192]{1,0:T(8,128)(2,1)} custom-call(bf16[512,128]{1,0:T(8,128)(2,1)S(1)} %bitcast.10, bf16[128,8192]{1,0:T(8,128)(2,1)S(1)} %bitcast.9, f32[1,8192]{1,0:T(1,128)S(1)} %bitcast.11), custom_call_target="tpu_custom_call" | custom-call | flops 1073741824 | bytes 8388608 | tf_op jit(solution)/shard_map/pallas_call | solution.py:298
  (4 shorter events, 0.1 us)
Async XLA Ops:
  2.4 8.7 %copy-start.1 = (bf16[2,2048,128]{2,1,0:T(8,128)(2,1)S(1)}, bf16[2,2048,128]{2,1,0:T(8,128)(2,1)}, u32[]{:S(2)}) copy-start(bf16[2,2048,128]{2,1,0:T(8,128)(2,1)} %mean_hbm.1) | copy-start | bytes 3145732
  2.4 8.7 %copy-start.2 = (f32[16,2048]{1,0:T(8,128)S(1)}, f32[16,2048]{1,0:T(8,128)}, u32[]{:S(2)}) copy-start(f32[16,2048]{1,0:T(8,128)} %frequencies.1) | copy-start | bytes 393220
  2.4 8.7 %copy-start.3 = (f32[512,16]{0,1:T(8,128)S(1)}, f32[512,16]{0,1:T(8,128)}, u32[]{:S(2)}) copy-start(f32[512,16]{0,1:T(8,128)} %param.9) | copy-start | bytes 98308
  2.4 8.7 %copy-start.4 = (f32[2048]{0:T(1024)S(1)}, f32[2048]{0:T(1024)}, u32[]{:S(2)}) copy-start(f32[2048]{0:T(1024)} %param.11) | copy-start | bytes 24580
  2.4 8.7 %copy-start.5 = (f32[128]{0:T(128)S(1)}, f32[128]{0:T(128)}, u32[]{:S(2)}) copy-start(f32[128]{0:T(128)} %param.12) | copy-start | bytes 1540
  2.5 8.7 %copy-start.6 = (f32[128]{0:T(128)S(1)}, f32[128]{0:T(128)}, u32[]{:S(2)}) copy-start(f32[128]{0:T(128)} %param.13) | copy-start | bytes 1540
  2.5 34.8 %all-to-all-start = ((bf16[8,16,8192]{2,1,0:T(8,128)(2,1)}), bf16[8,16,8192]{2,1,0:T(8,128)(2,1)S(1)}, u32[]{:S(2)}, u32[]{:S(2)}) async-start(bf16[8,16,8192]{2,1,0:T(8,128)(2,1)} %shard_map.91), calls=%async_computation | async-start | bytes 4194304 | tf_op jit(solution)/shard_map/all_to_all | solution.py:326
  25.1 38.8 %copy-start = (f32[8192]{0:T(1024)S(1)}, f32[8192]{0:T(1024)}, u32[]{:S(2)}) copy-start(f32[8192]{0:T(1024)} %param.17) | copy-start | bytes 98308
  25.1 2.2 %collective-permute-start = (f32[4,2,2,32,128]{4,3,2,1,0:T(8,128)S(1)}, f32[4,2,2,32,128]{4,3,2,1,0:T(8,128)S(1)}, u32[]{:S(2)}, u32[]{:S(2)}) collective-permute-start(f32[4,2,2,32,128]{4,3,2,1,0:T(8,128)S(1)} %get-tuple-element.14), channel_id=1, source_target_pairs={{0,8},{8,0},{1,9},{9,1},{2,10},{10,2},{3,11},{11,3},{4,12},{12,4},... | collective-permute-start | bytes 786440 | tf_op jit(solution)/shard_map/ppermute | solution.py:331
  27.3 3.9 %collective-permute-start.1 = (f32[2,2,32,128]{3,2,1,0:T(8,128)S(1)}, f32[2,2,32,128]{3,2,1,0:T(8,128)S(1)}, u32[]{:S(2)}, u32[]{:S(2)}) collective-permute-start(f32[2,2,32,128]{3,2,1,0:T(8,128)S(1)} %get-tuple-element.16), channel_id=1, source_target_pairs={{0,16},{16,0},{32,48},{48,32},{1,17},{17,1},{33,49},{49,33},{2,18}... | collective-permute-start | bytes 196616 | tf_op jit(solution)/shard_map/ppermute | solution.py:334
  28.6 5.7 %collective-permute-start.2 = (f32[2,2,32,128]{3,2,1,0:T(8,128)S(1)}, f32[2,2,32,128]{3,2,1,0:T(8,128)S(1)}, u32[]{:S(2)}, u32[]{:S(2)}) collective-permute-start(f32[2,2,32,128]{3,2,1,0:T(8,128)S(1)} %get-tuple-element.17), channel_id=1, source_target_pairs={{0,32},{16,48},{32,0},{48,16},{1,33},{17,49},{33,1},{49,17},{2,34}... | collective-permute-start | bytes 196616 | tf_op jit(solution)/shard_map/ppermute | solution.py:334
  31.1 4.8 %collective-permute-start.3 = (f32[2,2,32,128]{3,2,1,0:T(8,128)S(1)}, f32[2,2,32,128]{3,2,1,0:T(8,128)S(1)}, u32[]{:S(2)}, u32[]{:S(2)}) collective-permute-start(f32[2,2,32,128]{3,2,1,0:T(8,128)S(1)} %get-tuple-element.18), channel_id=1, source_target_pairs={{0,48},{16,32},{32,16},{48,0},{1,49},{17,33},{33,17},{49,1},{2,50}... | collective-permute-start | bytes 196616 | tf_op jit(solution)/shard_map/ppermute | solution.py:334
